TPU v7x, 32 devices: a whole 2x2x4 slice. The times are simulated.
32 devices in a mesh: rows: 16 (over z, x, core), chan: 2 (over y).
Axes of the slice: x: 2, y: 2, z: 4, core: 2. Of those that a mesh axis runs over, the one named last changes fastest.
Arguments:
- feature: bfloat16 [48, 144, 1536], P('rows', None, 'chan'), may hold values from -6 to 6
- kernel: float32 [7, 7, 1536], P(None, None, 'chan'), may hold values from -0.875 to 0.875
- ln_gain: float32 [1536], replicated, may hold values from 0.1 to 1.9
- layer_scale: float32 [1536], replicated, may hold values from 0.1 to 1.9
- w_in: bfloat16 [1536, 6144], P(None, 'chan'), may hold values from -0.15625 to 0.15625
- w_out: bfloat16 [6144, 1536], P('chan'), may hold values from -0.078125 to 0.078125
- cotangent: bfloat16 [48, 144, 1536], P('rows'), may hold values from -6 to 6
Outputs:
- grad_feature: bfloat16 [48, 144, 1536], P('rows', None, 'chan')
- grad_w_in: float32 [1536, 6144], P('rows', 'chan')
- grad_w_out: float32 [6144, 1536], P('chan', 'rows')
- grad_kernel: float32 [7, 7, 1536], P(None, None, 'chan')
All inputs are finite; a program needn't handle non-finite values.
Results may differ from a plain program's by a relative error of at most 0.03.
Values may be sent and summed in bfloat16 or wider, within the bound.
A program may use at most 128 MiB of HBM per device.

v0:
```python
import math

import jax
import jax.numpy as jnp
from jax import lax
from jax.sharding import PartitionSpec as P


def extended(cells, sides, width):
    for axis, dim in sides:
        count = lax.axis_size(axis)
        ends = count - 1
        head = lax.slice_in_dim(cells, 0, width, axis=dim)
        tail = lax.slice_in_dim(cells, cells.shape[dim] - width, cells.shape[dim], axis=dim)
        cells = jnp.concatenate(
            [
                lax.ppermute(tail, axis, [(i, (i + 1) % count) for i in range(ends)]),
                cells,
                lax.ppermute(head, axis, [((i + 1) % count, i) for i in range(ends)]),
            ],
            axis=dim,
        )
    return cells


def conv_taps(padded, kernel, height, width):
    result = jnp.zeros((height, width, kernel.shape[2]), jnp.float32)
    for tap_row in range(7):
        for tap_col in range(7):
            window = padded[tap_row : tap_row + height, tap_col : tap_col + width].astype(
                jnp.float32
            )
            result = result + window * kernel[tap_row, tap_col]
    return result


def conv_back(grad_pad, kernel, height, width):
    result = jnp.zeros((height, width, kernel.shape[2]), jnp.float32)
    for tap_row in range(7):
        for tap_col in range(7):
            window = grad_pad[
                6 - tap_row : 6 - tap_row + height, 6 - tap_col : 6 - tap_col + width
            ].astype(jnp.float32)
            result = result + window * kernel[tap_row, tap_col]
    return result


def kernel_terms(grad_conv, padded, height, width):
    grad_float = grad_conv.astype(jnp.float32)
    rows_list = []
    for tap_row in range(7):
        cols_list = []
        for tap_col in range(7):
            window = padded[tap_row : tap_row + height, tap_col : tap_col + width].astype(
                jnp.float32
            )
            cols_list.append(jnp.sum(grad_float * window, axis=(0, 1)))
        rows_list.append(jnp.stack(cols_list))
    return jnp.stack(rows_list)


def gelu_tanh(value):
    return jax.nn.gelu(value, approximate=True)


def shards(feature, kernel, ln_gain, layer_scale, w_in, w_out, cotangent):
    height, width, local_ch = feature.shape
    channels = cotangent.shape[2]
    pixels = height * width
    scale = 1.0 / math.sqrt(height * lax.axis_size("rows") * width)
    offset = lax.axis_index("chan") * local_ch
    rimmed = extended(feature, (("rows", 0),), 3)
    padded = jnp.pad(rimmed, ((0, 0), (3, 3), (0, 0)))
    conv_local = conv_taps(padded, kernel, height, width).astype(jnp.bfloat16)
    conv_full = lax.all_gather(conv_local, "chan", axis=2, tiled=True)
    values = conv_full.reshape(pixels, channels).astype(jnp.float32)
    mean = jnp.mean(values, axis=1, keepdims=True)
    centred = values - mean
    var = jnp.mean(centred * centred, axis=1, keepdims=True)
    rstd = 1.0 / jnp.sqrt(var + 1e-06)
    nhat = centred * rstd
    normed = (nhat * ln_gain).astype(jnp.bfloat16)
    hidden = jnp.dot(normed, w_in, preferred_element_type=jnp.float32)
    activ = gelu_tanh(hidden).astype(jnp.bfloat16)
    grad_mixed = (cotangent.reshape(pixels, channels).astype(jnp.float32) * layer_scale).astype(
        jnp.bfloat16
    )
    grad_activ = lax.dot_general(
        grad_mixed, w_out, (((1,), (1,)), ((), ())), preferred_element_type=jnp.float32
    )
    grad_hidden = jax.vjp(gelu_tanh, hidden)[1](grad_activ)[0].astype(jnp.bfloat16)
    part_out = (
        lax.dot_general(
            activ, grad_mixed, (((0,), (0,)), ((), ())), preferred_element_type=jnp.float32
        )
        * scale
    )
    grad_w_in = lax.psum_scatter(
        (
            lax.dot_general(
                normed, grad_hidden, (((0,), (0,)), ((), ())), preferred_element_type=jnp.float32
            )
            * scale
        ).astype(jnp.bfloat16),
        "rows",
        scatter_dimension=0,
        tiled=True,
    ).astype(jnp.float32)
    grad_w_out = lax.psum_scatter(
        part_out.astype(jnp.bfloat16), "rows", scatter_dimension=1, tiled=True
    ).astype(jnp.float32)
    nhat_own = lax.dynamic_slice_in_dim(nhat, offset, local_ch, 1)
    grad_normed = lax.psum(
        lax.dot_general(
            grad_hidden, w_in, (((1,), (1,)), ((), ())), preferred_element_type=jnp.float32
        ).astype(jnp.bfloat16),
        "chan",
    ).astype(jnp.float32)
    scaled_full = grad_normed * ln_gain
    first_mean = jnp.mean(scaled_full, axis=1, keepdims=True)
    second_mean = jnp.mean(scaled_full * nhat, axis=1, keepdims=True)
    scaled = lax.dynamic_slice_in_dim(scaled_full, offset, local_ch, 1)
    grad_local = rstd * (scaled - first_mean - nhat_own * second_mean)
    grad_conv = grad_local.astype(jnp.bfloat16).reshape(height, width, local_ch)
    grad_rimmed = extended(grad_conv, (("rows", 0),), 3)
    grad_pad = jnp.pad(grad_rimmed, ((0, 0), (3, 3), (0, 0)))
    cot_own = lax.dynamic_slice_in_dim(cotangent, offset, local_ch, 2).astype(jnp.float32)
    grad_feature = (cot_own + conv_back(grad_pad, kernel, height, width)).astype(jnp.bfloat16)
    kernel_part = kernel_terms(grad_conv, padded, height, width) * scale
    grad_kernel = lax.psum(kernel_part.astype(jnp.bfloat16), "rows").astype(jnp.float32)
    return (grad_feature, grad_w_in, grad_w_out, grad_kernel)


def solution(mesh):
    placed = (
        P("rows", None, "chan"),
        P(None, None, "chan"),
        P(),
        P(),
        P(None, "chan"),
        P("chan", None),
        P("rows", None, None),
    )
    return jax.shard_map(
        shards,
        mesh=mesh,
        in_specs=placed,
        out_specs=(
            P("rows", None, "chan"),
            P("rows", "chan"),
            P("chan", "rows"),
            P(None, None, "chan"),
        ),
        check_vma=False,
    )
```

profile of v0, /device:TPU:0, one launch (start us, length us, event | category | flops | bytes accessed | tf_op | source)
XLA Modules:
  0.0 480.6 jit_solution(14458472323641660062)
XLA Ops:
  7.2 0.0 all-gather.2.cloned.1.call-start
  7.2 2.5 collective-permute-start
  9.8 1.3 collective-permute-start.1
  11.1 1.1 slice_reduce_fusion.46
  12.1 1.5 slice_reduce_fusion.48
  13.6 1.4 slice_reduce_fusion.47
  15.3 0.1 constant_dynamic-update-slice_fusion
  15.4 0.7 collective-permute-done.1
  16.0 0.7 fusion.18
  17.0 0.9 copy-done.8
  17.9 10.4 %fusion.141 = bf16[3,144,768]{2,1,0:T(8,128)(2,1)} fusion(bf16[3,144,768]{2,1,0:T(8,128)(2,1)S(1)} %collective-permute-done.1, bf16[3,144,768]{2,1,0:T(8,128)(2,1)S(1)} %copy-done.3, bf16[3,144,768]{2,1,0:T(8,128)(2,1)S(1)} %collective-permute-done, f32[768]{0:T(1024)S(1)} %get-tuple-element.106, f32[768]{0:T(1024)S(1)} %get-tuple-element.107, ...), kind=kLoop, calls=%fused_computation.263 | loop fusion | flops 48771072 | bytes 33328128 | tf_op jit(solution)/shard_map/convert_element_type | solution.py:74
  28.3 0.2 all-reduce.5.cloned.1.call-start
  28.5 1.5 fusion.8
  30.1 1.1 copy-done.13
  31.2 11.1 %fusion.150 = f32[432,3072]{1,0:T(8,128)} fusion(bf16[432,1536]{1,0:T(8,128)(2,1)S(1)} %fusion.8, bf16[3072,1536]{1,0:T(8,128)(2,1)} %param.12), kind=kOutput, calls=%fused_computation.339 | convolution fusion | flops 4076863488 | bytes 16072704 | tf_op jit(solution)/shard_map/dot_general | solution.py:88
  42.2 23.4 %all-gather.2.cloned.1.call-done = bf16[3,144,1536]{2,1,0:T(8,128)(2,1)} async-done(((bf16[3,144,768]{2,1,0:T(8,128)(2,1)}), bf16[3,144,1536]{2,1,0:T(8,128)(2,1)}) %all-gather.2.cloned.1.call-update) | async-done | bytes 1327120 | tf_op jit(solution)/shard_map/all_gather | solution.py:75
  65.7 1.6 convert_reduce_fusion
  67.3 0.1 div.18
  67.3 1.8 multiply_reduce_fusion.1
  69.2 0.1 sqrt.6
  69.3 1.8 fusion.9
  71.2 14.6 %fusion.6 = (bf16[432,3072]{1,0:T(8,128)(2,1)S(1)}, f32[432,3072]{1,0:T(8,128)}) fusion(f32[432,3072]{1,0:T(8,128)} %fusion.150, bf16[1536,3072]{1,0:T(8,128)(2,1)} %param.11, f32[432,1536]{1,0:T(8,128)S(1)} %fusion.9, f32[1536]{0:T(1024)S(1)} %copy-done.53), kind=kOutput, calls=%fused_computation.62 | convolution fusion | flops 4104732672 | bytes 25368576 | tf_op jit(solution)/shard_map/dot_general | solution.py:83
  85.8 1.5 copy-done.55
  87.3 5.4 %convolution_convert_fusion = bf16[432,1536]{1,0:T(8,128)(2,1)} fusion(bf16[432,3072]{1,0:T(8,128)(2,1)S(1)} %get-tuple-element.111, bf16[1536,3072]{1,0:T(8,128)(2,1)S(1)} %bitcast.37), kind=kOutput, calls=%fused_computation.65 | convolution fusion | flops 4077527040 | bytes 13418496 | tf_op jit(solution)/shard_map/dot_general | solution.py:114
  92.7 0.3 all-reduce.7.cloned.1.call-start
  93.0 46.0 %all-reduce.5.cloned.1.call-done = bf16[432,1536]{1,0:T(8,128)(2,1)} async-done(((bf16[432,1536]{1,0:T(8,128)(2,1)}), bf16[432,1536]{1,0:T(8,128)(2,1)}) %all-reduce.5.cloned.1.call-update) | async-done | bytes 1327120 | tf_op jit(solution)/shard_map/psum | solution.py:113
  139.0 3.0 fusion.142
  142.1 0.3 multiply_convert_fusion.5
  142.3 3.2 fusion.139
  145.6 3.3 fusion.140
  148.9 2.1 fusion.138
  152.0 0.7 multiply_convert_fusion.8
  152.7 0.0 reduce-scatter.5.cloned.1.call-start
  152.8 10.8 %multiply_convert_fusion = bf16[3072,1536]{0,1:T(8,128)(2,1)} fusion(bf16[432,1536]{1,0:T(8,128)(2,1)S(1)} %copy-done.14, f32[432,3072]{1,0:T(8,128)} %get-tuple-element.112), kind=kOutput, calls=%fused_computation | convolution fusion | flops 4098244608 | bytes 16072704 | tf_op jit(solution)/shard_map/dot_general | solution.py:93
  163.5 0.0 reduce-scatter.3.cloned.1.call-start
  163.6 1.7 copy-done.2
  165.3 9.3 %multiply_convert_fusion.1 = bf16[1536,3072]{1,0:T(8,128)(2,1)} fusion(bf16[432,3072]{1,0:T(8,128)(2,1)} %copy-done.55, f32[432,1536]{1,0:T(8,128)S(1)} %copy-done.2, f32[1536]{0:T(1024)S(1)} %copy-done.54), kind=kOutput, calls=%fused_computation.1 | convolution fusion | flops 4087627776 | bytes 14751744 | tf_op jit(solution)/shard_map/dot_general | solution.py:100
  174.6 1.3 collective-permute-start.3
  175.9 3.3 collective-permute-start.2
  179.2 61.0 %all-reduce.7.cloned.1.call-done = bf16[7,7,768]{2,1,0:T(8,128)(2,1)} async-done(((bf16[7,7,768]{2,1,0:T(8,128)(2,1)}), bf16[7,7,768]{2,1,0:T(8,128)(2,1)}) %all-reduce.7.cloned.1.call-update) | async-done | bytes 75280 | tf_op jit(solution)/shard_map/psum | solution.py:130
  240.2 1.6 convert_element_type.529
  242.0 0.7 select_maximum_fusion
  242.7 0.4 copy-done.12
  243.3 10.7 %add_convert_fusion = bf16[3,144,768]{2,1,0:T(8,128)(2,1)} fusion(bf16[3,144,768]{2,1,0:T(8,128)(2,1)S(1)} %collective-permute-done.2, bf16[3,144,768]{2,1,0:T(8,128)(2,1)S(1)} %bitcast.35, bf16[3,144,768]{2,1,0:T(8,128)(2,1)S(1)} %collective-permute-done.3, bf16[9,150,768]{2,1,0:T(8,128)(2,1)S(1)} %select_maximum_fusion, f32[768]{0:T(1024)S(1)} %get-tuple-element.106, ...), kind=kLoop, calls=%fused_computation.260 | loop fusion | flops 53415936 | bytes 31337476 | tf_op jit(solution)/shard_map/convert_element_type | solution.py:128
  254.0 102.3 %reduce-scatter.5.cloned.1.call-done = bf16[3072,96]{0,1:T(8,128)(2,1)} async-done(((bf16[3072,1536]{0,1:T(8,128)(2,1)}), bf16[3072,96]{0,1:T(8,128)(2,1)}) %reduce-scatter.5.cloned.1.call-update) | async-done | bytes 589840 | tf_op jit(solution)/shard_map/reduce_scatter | solution.py:109
  356.2 2.2 convert_element_type.527
  358.4 113.4 %reduce-scatter.3.cloned.1.call-done = bf16[96,3072]{1,0:T(8,128)(2,1)} async-done(((bf16[1536,3072]{1,0:T(8,128)(2,1)}), bf16[96,3072]{1,0:T(8,128)(2,1)}) %reduce-scatter.3.cloned.1.call-update) | async-done | bytes 589840 | tf_op jit(solution)/shard_map/reduce_scatter | solution.py:98
  471.9 2.2 convert_element_type.524
  (190 shorter events, 1.0 us)
Async XLA Ops:
  7.2 8.1 %copy-start.3 = (bf16[3,144,768]{2,1,0:T(8,128)(2,1)S(1)}, bf16[3,144,768]{2,1,0:T(8,128)(2,1)}, u32[]{:S(2)}) copy-start(bf16[3,144,768]{2,1,0:T(8,128)(2,1)} %param.7) | copy-start | bytes 1990660
  7.2 58.5 %all-gather.2.cloned.1.call-start = ((), (), s32[]{:S(2)}) async-start(), calls=%async_computation.2 | async-start | bytes 1990656 | tf_op jit(solution)/shard_map/all_gather | solution.py:75
  7.2 8.0 %collective-permute-start = (bf16[3,144,768]{2,1,0:T(8,128)(2,1)}, bf16[3,144,768]{2,1,0:T(8,128)(2,1)S(1)}, u32[]{:S(2)}, u32[]{:S(2)}) collective-permute-start(bf16[3,144,768]{2,1,0:T(8,128)(2,1)} %param.7), channel_id=1, source_target_pairs={{0,2},{2,4},{4,6},{6,8},{8,10},{10,12},{12,14},{14,16},{16,18},{18... | collective-permute-start | bytes 1990664 | tf_op jit(solution)/shard_map/ppermute | solution.py:17
  9.8 6.3 %collective-permute-start.1 = (bf16[3,144,768]{2,1,0:T(8,128)(2,1)}, bf16[3,144,768]{2,1,0:T(8,128)(2,1)S(1)}, u32[]{:S(2)}, u32[]{:S(2)}) collective-permute-start(bf16[3,144,768]{2,1,0:T(8,128)(2,1)} %param.7), channel_id=1, source_target_pairs={{2,0},{4,2},{6,4},{8,6},{10,8},{12,10},{14,12},{16,14},{18,16},{20... | collective-permute-start | bytes 1990664 | tf_op jit(solution)/shard_map/ppermute | solution.py:19
  15.0 1.8 copy-start.15
  15.0 1.8 copy-start.17
  15.0 1.8 copy-start.19
  15.0 1.8 copy-start.21
  15.0 1.8 copy-start.23
  15.1 1.8 copy-start.25
  15.1 1.8 copy-start.27
  15.1 1.8 copy-start.29
  15.1 1.8 copy-start.31
  15.1 1.8 copy-start.33
  15.1 1.8 copy-start.35
  15.1 1.8 copy-start.37
  15.1 1.8 copy-start.39
  15.1 1.8 copy-start.41
  15.1 1.8 copy-start.43
  15.2 1.8 copy-start.45
  15.2 1.8 copy-start.47
  15.2 1.8 copy-start.49
  15.2 1.8 copy-start.4
  15.4 1.7 copy-start.10
  28.3 110.7 %all-reduce.5.cloned.1.call-start = ((), (), s32[]{:S(2)}) async-start(), calls=%async_computation.3 | async-start | bytes 2654208 | tf_op jit(solution)/shard_map/psum | solution.py:113
  69.3 1.8 copy-start.51
  69.3 1.8 copy-start.53
  69.3 18.0 %slice-start = ((s8[9437184]{0:T(1024)(128)(4,1)}), s8[4194304]{0:T(1024)(128)(4,1)S(1)}, s32[]{:S(2)}) async-start(s8[9437184]{0:T(1024)(128)(4,1)} %bitcast.36), calls=%async_computation.7 | async-start | bytes 8388608
  71.1 14.6 %copy-start = (f32[432,1536]{1,0:T(8,128)}, f32[432,1536]{1,0:T(8,128)S(1)}, u32[]{:S(2)}) copy-start(f32[432,1536]{1,0:T(8,128)S(1)} %fusion.9) | copy-start | bytes 7962628
  71.2 16.1 %slice-start.1 = ((s8[9437184]{0:T(1024)(128)(4,1)}), s8[4194304]{0:T(1024)(128)(4,1)S(1)}, s32[]{:S(2)}) async-start(s8[9437184]{0:T(1024)(128)(4,1)} %bitcast.36), calls=%async_computation.8 | async-start | bytes 8388608
  71.2 16.1 %slice-start.2 = ((s8[9437184]{0:T(1024)(128)(4,1)}), s8[1048576]{0:T(1024)(128)(4,1)S(1)}, s32[]{:S(2)}) async-start(s8[9437184]{0:T(1024)(128)(4,1)} %bitcast.36), calls=%async_computation.9 | async-start | bytes 2097152
  85.8 1.5 copy-start.55
  92.7 147.5 %all-reduce.7.cloned.1.call-start = ((), (), s32[]{:S(2)}) async-start(), calls=%async_computation.6 | async-start | bytes 172032 | tf_op jit(solution)/shard_map/psum | solution.py:130
  139.0 3.0 copy-start.1
  139.0 3.0 copy-start.52
  145.5 3.3 copy-start.5
  145.6 3.3 copy-start.7
  145.6 3.3 copy-start.9
  145.6 3.3 copy-start.11
  151.0 1.8 copy-start.14
  152.7 203.5 %reduce-scatter.5.cloned.1.call-start = ((), (), s32[]{:S(2)}) async-start(), calls=%async_computation.5 | async-start | bytes 10027008 | tf_op jit(solution)/shard_map/reduce_scatter | solution.py:109
  163.5 1.8 copy-start.2
  163.5 1.8 copy-start.54
  163.5 308.3 %reduce-scatter.3.cloned.1.call-start = ((), (), s32[]{:S(2)}) async-start(), calls=%async_computation.4 | async-start | bytes 10027008 | tf_op jit(solution)/shard_map/reduce_scatter | solution.py:98
  174.6 67.4 %collective-permute-start.3 = (bf16[3,144,768]{2,1,0:T(8,128)(2,1)S(1)}, bf16[3,144,768]{2,1,0:T(8,128)(2,1)S(1)}, u32[]{:S(2)}, u32[]{:S(2)}) collective-permute-start(bf16[3,144,768]{2,1,0:T(8,128)(2,1)S(1)} %bitcast.32), channel_id=1, source_target_pairs={{2,0},{4,2},{6,4},{8,6},{10,8},{12,10},{14,12},{16,14},{18,16},{20... | collective-permute-start | bytes 1990664 | tf_op jit(solution)/shard_map/ppermute | solution.py:19
  175.9 66.1 %collective-permute-start.2 = (bf16[3,144,768]{2,1,0:T(8,128)(2,1)S(1)}, bf16[3,144,768]{2,1,0:T(8,128)(2,1)S(1)}, u32[]{:S(2)}, u32[]{:S(2)}) collective-permute-start(bf16[3,144,768]{2,1,0:T(8,128)(2,1)S(1)} %bitcast.33), channel_id=1, source_target_pairs={{0,2},{2,4},{4,6},{6,8},{8,10},{10,12},{12,14},{14,16},{16,18},{18... | collective-permute-start | bytes 1990664 | tf_op jit(solution)/shard_map/ppermute | solution.py:17
  241.8 1.3 copy-start.18
  241.8 1.3 copy-start.20
  (20 other events, 25.6 us)
Sparse Core Ops, SparseCore 0:
  28.4 37.1 all-gather.1
  92.9 46.1 all-reduce.4
  152.8 87.3 all-reduce.6
  244.2 111.9 reduce-scatter.4
  360.7 111.0 reduce-scatter.2
where the time goes:
time: 481 us
  waiting for transfers between devices  347 us (72%)
  matrix products  51.2 us (11%)
  other arithmetic  47.7 us (10%)
  between operations  15.1 us (3%)
  local copies, waits for them, and re-layouts  10.6 us (2%)
  starting transfers between devices  9.05 us (2%)
    reduce_scatter x1, waiting for transfers between devices, shards(): lax.psum_scatter((lax.dot_general(normed, grad_hidden, (((0,), (0,)), (()...  113 us
    reduce_scatter x1, waiting for transfers between devices, shards(): lax.psum_scatter(part_out.astype(jnp.bfloat16), 'rows', scatter_dimension...  102 us
    psum x1, waiting for transfers between devices, shards(): lax.psum(kernel_part.astype(jnp.bfloat16), 'rows').astype(jnp.float32)  61 us
    psum x1, waiting for transfers between devices, shards(): lax.psum(lax.dot_general(grad_hidden, w_in, (((1,), (1,)), ((), ())), pre...  46 us
    all_gather x1, waiting for transfers between devices, shards(): conv_full = lax.all_gather(conv_local, 'chan', axis=2, tiled=True)  23.4 us
    dot_general x1, matrix products, shards(): hidden = jnp.dot(normed, w_in, preferred_element_type=jnp.float32)  14.6 us
    dot_general x1, matrix products, shards(): lax.dot_general(grad_mixed, w_out, (((1,), (1,)), ((), ())), preferred_el...  11.1 us
    dot_general x1, matrix products, shards(): lax.dot_general(activ, grad_mixed, (((0,), (0,)), ((), ())), preferred_el...  10.8 us
  transfers between devices with their start and end apart: 9, of which 6 were waited for; matrix products, arithmetic and copies ran while one was open for 11% of the time, Pallas kernels for 0%

commit v1 on v0

v1 whole, which is shorter than its diff:
```python
import math

import jax
import jax.numpy as jnp
from jax import lax
from jax.sharding import PartitionSpec as P


def halo(cells, width):
    count = lax.axis_size("rows")
    ends = count - 1
    head = cells[:width]
    tail = cells[cells.shape[0] - width :]
    above = lax.ppermute(tail, "rows", [(i, i + 1) for i in range(ends)])
    below = lax.ppermute(head, "rows", [(i + 1, i) for i in range(ends)])
    return jnp.concatenate([above, cells, below], axis=0)


def conv_taps(padded, kernel, height, width):
    result = jnp.zeros((height, width, kernel.shape[2]), jnp.float32)
    for tap_row in range(7):
        for tap_col in range(7):
            window = padded[tap_row : tap_row + height, tap_col : tap_col + width].astype(
                jnp.float32
            )
            result = result + window * kernel[tap_row, tap_col]
    return result


def conv_back(grad_pad, kernel, height, width):
    result = jnp.zeros((height, width, kernel.shape[2]), jnp.float32)
    for tap_row in range(7):
        for tap_col in range(7):
            window = grad_pad[
                6 - tap_row : 6 - tap_row + height, 6 - tap_col : 6 - tap_col + width
            ].astype(jnp.float32)
            result = result + window * kernel[tap_row, tap_col]
    return result


def kernel_terms(grad_conv, padded, height, width):
    grad_float = grad_conv.astype(jnp.float32)
    rows_list = []
    for tap_row in range(7):
        cols_list = []
        for tap_col in range(7):
            window = padded[tap_row : tap_row + height, tap_col : tap_col + width].astype(
                jnp.float32
            )
            cols_list.append(jnp.sum(grad_float * window, axis=(0, 1)))
        rows_list.append(jnp.stack(cols_list))
    return jnp.stack(rows_list)


def gelu_tanh(value):
    return jax.nn.gelu(value, approximate=True)


def chip_at(place, chips):
    place = place % chips
    half = chips // 2
    return jnp.where(place < half, 2 * place, 2 * (chips - 1 - place) + 1)


def ring_pairs(chips, step):
    def chip(place):
        place = place % chips
        half = chips // 2
        return 2 * place if place < half else 2 * (chips - 1 - place) + 1

    return [
        (2 * chip(p) + core, 2 * chip(p + step) + core) for p in range(chips) for core in range(2)
    ]


def ring_sums(part, place, chips):
    share = part.shape[0] // chips
    half = share // 2

    def piece(position, side):
        return lax.dynamic_slice_in_dim(
            part, chip_at(position, chips) * share + side * half, half, 0
        )

    sums = [piece(place + chips - 1, 0), piece(place + 1, 1)]
    for step in range(chips - 1):
        for side, way in ((0, 1), (1, -1)):
            got = lax.ppermute(sums[side], "rows", ring_pairs(chips, way))
            own = piece(place + 2 * chips - way * (2 + step), side)
            total = got.astype(jnp.float32) + own.astype(jnp.float32)
            sums[side] = total.astype(jnp.bfloat16)
    return sums


def own_rows(sums, core, swap):
    mine = jnp.where(core == 0, sums[0], sums[1])
    theirs = jnp.where(core == 0, sums[1], sums[0])
    got = lax.ppermute(theirs, "rows", swap)
    first = jnp.where(core == 0, mine, got)
    second = jnp.where(core == 0, got, mine)
    return jnp.concatenate([first, second], axis=1).astype(jnp.float32)


def shards(feature, kernel, ln_gain, layer_scale, w_in, w_out, cotangent):
    height, width, local_ch = feature.shape
    channels = cotangent.shape[2]
    pixels = height * width
    rows = lax.axis_size("rows")
    chan = lax.axis_size("chan")
    chips = rows // 2
    me = lax.axis_index("rows")
    lane = lax.axis_index("chan")
    core = me % 2
    chip = me // 2
    place = jnp.where(chip % 2 == 0, chip // 2, chips - 1 - chip // 2)
    swap = [(i, i ^ 1) for i in range(rows)]
    cross = [(0, 1), (1, 0)]
    scale = 1.0 / math.sqrt(height * rows * width)
    offset = lane * local_ch
    units = w_in.shape[1] // 2

    rimmed = halo(feature, 3)
    grad_mixed = (cotangent.reshape(pixels, channels).astype(jnp.float32) * layer_scale).astype(
        jnp.bfloat16
    )
    mixed_both = jnp.concatenate([grad_mixed, lax.ppermute(grad_mixed, "rows", swap)], axis=0)
    in_part = lax.dynamic_slice_in_dim(w_in, core * units, units, 1)
    out_part = lax.dynamic_slice_in_dim(w_out, core * units, units, 0)

    padded = jnp.pad(rimmed, ((0, 0), (3, 3), (0, 0)))
    conv_local = conv_taps(padded, kernel, height, width).astype(jnp.bfloat16)
    conv_local = conv_local.reshape(pixels, local_ch)
    if chan == 2:
        conv_other = lax.ppermute(conv_local, "chan", cross)
        conv_full = jnp.concatenate(
            [
                jnp.where(lane == 0, conv_local, conv_other),
                jnp.where(lane == 0, conv_other, conv_local),
            ],
            axis=1,
        )
    else:
        conv_full = lax.all_gather(conv_local, "chan", axis=1, tiled=True)
    grad_activ = lax.dot_general(
        mixed_both, out_part, (((1,), (1,)), ((), ())), preferred_element_type=jnp.float32
    )
    values = conv_full.astype(jnp.float32)
    mean = jnp.mean(values, axis=1, keepdims=True)
    centred = values - mean
    var = jnp.mean(centred * centred, axis=1, keepdims=True)
    rstd = 1.0 / jnp.sqrt(var + 1e-06)
    nhat = centred * rstd
    normed = (nhat * ln_gain).astype(jnp.bfloat16)
    normed_both = jnp.concatenate([normed, lax.ppermute(normed, "rows", swap)], axis=0)
    hidden = jnp.dot(normed_both, in_part, preferred_element_type=jnp.float32)
    activ = gelu_tanh(hidden).astype(jnp.bfloat16)
    grad_hidden = jax.vjp(gelu_tanh, hidden)[1](grad_activ)[0].astype(jnp.bfloat16)

    def pixel_sum(left, right):
        total = lax.dot_general(
            left, right, (((0,), (0,)), ((), ())), preferred_element_type=jnp.float32
        )
        return (total * scale).astype(jnp.bfloat16)

    def back(grads):
        return lax.dot_general(
            grads, in_part, (((1,), (1,)), ((), ())), preferred_element_type=jnp.float32
        )

    out_sums = ring_sums(pixel_sum(mixed_both, activ), place, chips)
    back_other = lax.ppermute(back(grad_hidden[pixels:]).astype(jnp.bfloat16), "rows", swap)
    back_own = back(grad_hidden[:pixels]) + back_other.astype(jnp.float32)
    in_sums = ring_sums(pixel_sum(normed_both, grad_hidden), place, chips)

    scaled_part = back_own * ln_gain
    first_part = jnp.sum(scaled_part, axis=1)
    second_part = jnp.sum(scaled_part * nhat, axis=1)
    pair = jnp.stack([first_part, second_part])
    if chan == 2:
        kept = lax.dynamic_slice_in_dim(back_own, offset, local_ch, 1)
        given = lax.dynamic_slice_in_dim(back_own, local_ch - offset, local_ch, 1)
        got = lax.ppermute(given.astype(jnp.bfloat16), "chan", cross).astype(jnp.float32)
        grad_normed = kept + got
        pair = pair + lax.ppermute(pair, "chan", cross)
    else:
        grad_normed = lax.psum_scatter(
            back_own.astype(jnp.bfloat16), "chan", scatter_dimension=1, tiled=True
        ).astype(jnp.float32)
        pair = lax.psum(pair, "chan")
    first_mean = pair[0][:, None] / channels
    second_mean = pair[1][:, None] / channels
    nhat_own = (conv_local.astype(jnp.float32) - mean) * rstd
    scaled = grad_normed * lax.dynamic_slice_in_dim(ln_gain, offset, local_ch, 0)
    grad_local = rstd * (scaled - first_mean - nhat_own * second_mean)
    grad_conv = grad_local.astype(jnp.bfloat16).reshape(height, width, local_ch)
    grad_rimmed = halo(grad_conv, 3)
    kernel_sum = (kernel_terms(grad_conv, padded, height, width) * scale).astype(jnp.bfloat16)
    grad_pad = jnp.pad(grad_rimmed, ((0, 0), (3, 3), (0, 0)))
    cot_own = lax.dynamic_slice_in_dim(cotangent, offset, local_ch, 2).astype(jnp.float32)
    grad_feature = (cot_own + conv_back(grad_pad, kernel, height, width)).astype(jnp.bfloat16)
    span = 1
    while span < rows:
        other = lax.ppermute(kernel_sum, "rows", [(i, i ^ span) for i in range(rows)])
        total = kernel_sum.astype(jnp.float32) + other.astype(jnp.float32)
        span *= 2
        kernel_sum = total if span >= rows else total.astype(jnp.bfloat16)
    grad_w_out = own_rows(out_sums, core, swap).T
    grad_w_in = own_rows(in_sums, core, swap)
    return (grad_feature, grad_w_in, grad_w_out, kernel_sum)


def solution(mesh):
    placed = (
        P("rows", None, "chan"),
        P(None, None, "chan"),
        P(),
        P(),
        P(None, "chan"),
        P("chan", None),
        P("rows", None, None),
    )
    return jax.shard_map(
        shards,
        mesh=mesh,
        in_specs=placed,
        out_specs=(
            P("rows", None, "chan"),
            P("rows", "chan"),
            P("chan", "rows"),
            P(None, None, "chan"),
        ),
        check_vma=False,
    )
```

time: 481 us -> 229 us (0.48)
  waiting for transfers between devices: 347 us -> 64.4 us
  starting transfers between devices: 9.05 us -> 66.6 us
  between operations: 15.1 us -> 2.33 us
  matrix products: 51.2 us -> 38.7 us
    reduce_scatter x2 -> x0, waiting for transfers between devices: 216 us -> none  [the longest x1 113 us: shards(): lax.psum_scatter((lax.dot_general(normed, grad_hidden, (((0,), (0,)), (()...]
    psum x2 -> x0, waiting for transfers between devices: 107 us -> none  [the longest x1 61 us: shards(): lax.psum(kernel_part.astype(jnp.bfloat16), 'rows').astype(jnp.float32)]
    ppermute x4 -> x44, waiting for transfers between devices: 0.67 us -> 64.4 us  [the longest x28 31 us: ring_sums(): got = lax.ppermute(sums[side], 'rows', ring_pairs(chips, way))]
    ppermute x4 -> x44, starting transfers between devices: 8.45 us -> 66.6 us  [the longest x28 33.9 us: ring_sums(): got = lax.ppermute(sums[side], 'rows', ring_pairs(chips, way))]
    all_gather x1 -> x0, waiting for transfers between devices: 23.4 us -> none  [shards(): conv_full = lax.all_gather(conv_local, 'chan', axis=2, tiled=True)]
    dot_general x5 -> x6, matrix products: 51.2 us -> 38.7 us  [the longest x2 15.3 us: pixel_sum(): lax.dot_general(left, right, (((0,), (0,)), ((), ())), preferred_element_...]
    unnamed x125 -> x131, local copies, waits for them, and re-layouts: 5.81 us -> 0.75 us
  transfers between devices with their start and end apart: 9 -> 44, of which waited for: 6 -> 22; matrix products, arithmetic and copies ran while one was open for 11% -> 24% of each run, Pallas kernels for 0% -> 0%
where the time goes in v1:
time: 229 us
  starting transfers between devices  66.6 us (29%)
  waiting for transfers between devices  64.4 us (28%)
  other arithmetic  49.6 us (22%)
  matrix products  38.7 us (17%)
  local copies, waits for them, and re-layouts  6.94 us (3%)
  between operations  2.33 us (1%)
    ppermute x28, starting transfers between devices, ring_sums(): got = lax.ppermute(sums[side], 'rows', ring_pairs(chips, way))  33.9 us
    ppermute x28, waiting for transfers between devices, ring_sums(): got = lax.ppermute(sums[side], 'rows', ring_pairs(chips, way))  31 us
    ppermute x4, waiting for transfers between devices, shards(): lax.ppermute(kernel_sum, 'rows', [(i, i ^ span) for i in range(rows)])  16.4 us
    dot_general x2, matrix products, pixel_sum(): lax.dot_general(left, right, (((0,), (0,)), ((), ())), preferred_element_...  15.3 us
    dot_general x1, matrix products, shards(): lax.dot_general(mixed_both, out_part, (((1,), (1,)), ((), ())), preferred...  11.4 us
    convert_element_type x1, other arithmetic, shards(): (cot_own + conv_back(grad_pad, kernel, height, width)).astype(jnp.bfloat16)  10.7 us
    ppermute x1, starting transfers between devices, shards(): lax.ppermute(normed, 'rows', swap)  10.5 us
    convert_element_type x1, other arithmetic, shards(): conv_local = conv_taps(padded, kernel, height, width).astype(jnp.bfloat16)  10.5 us
  transfers between devices with their start and end apart: 44, of which 22 were waited for; matrix products, arithmetic and copies ran while one was open for 24% of the time, Pallas kernels for 0%

profile of v1, /device:TPU:0, one launch (start us, length us, event | category | flops | bytes accessed | tf_op | source)
XLA Modules:
  0.0 228.6 jit_solution(17373638862466518071)
XLA Ops:
  0.6 2.5 %collective-permute-start = (bf16[3,144,768]{2,1,0:T(8,128)(2,1)}, bf16[3,144,768]{2,1,0:T(8,128)(2,1)S(1)}, u32[]{:S(2)}, u32[]{:S(2)}) collective-permute-start(bf16[3,144,768]{2,1,0:T(8,128)(2,1)} %param.7), channel_id=1, source_target_pairs={{0,2},{2,4},{4,6},{6,8},{8,10},{10,12},{12,14},{14,16},{16,18},{18... | collective-permute-start | bytes 1990664 | tf_op jit(solution)/shard_map/ppermute | solution.py:14
  5.6 1.4 slice_reduce_fusion.48
  7.0 1.4 slice_reduce_fusion.47
  10.5 10.5 %fusion.168 = bf16[3,144,768]{2,1,0:T(8,128)(2,1)} fusion(bf16[3,144,768]{2,1,0:T(8,128)(2,1)S(1)} %collective-permute-done.1, bf16[3,144,768]{2,1,0:T(8,128)(2,1)S(1)} %copy-done, bf16[3,144,768]{2,1,0:T(8,128)(2,1)S(1)} %collective-permute-done, f32[768]{0:T(1024)S(1)} %get-tuple-element.106, f32[768]{0:T(1024)S(1)} %get-tuple-element.107, ...), kind=kLoop, calls=%fused_computation.283 | loop fusion | flops 48771072 | bytes 33328128 | tf_op jit(solution)/shard_map/convert_element_type | solution.py:131
  21.0 1.9 collective-permute-start.2
  22.9 9.1 %collective-permute-done.2 = bf16[432,768]{1,0:T(8,128)(2,1)} collective-permute-done((bf16[432,768]{1,0:T(8,128)(2,1)}, bf16[432,768]{1,0:T(8,128)(2,1)}, u32[]{:S(2)}, u32[]{:S(2)}) %collective-permute-start.2) | collective-permute-done | bytes 663584 | tf_op jit(solution)/shard_map/ppermute | solution.py:134
  34.2 1.6 fusion.27
  35.8 10.5 %collective-permute-start.4 = (bf16[432,1536]{1,0:T(8,128)(2,1)}, bf16[432,1536]{1,0:T(8,128)(2,1)}, u32[]{:S(2)}, u32[]{:S(2)}) collective-permute-start(bf16[432,1536]{1,0:T(8,128)(2,1)} %fusion.27), channel_id=1, source_target_pairs={{0,2},{2,0},{4,6},{6,4},{8,10},{10,8},{12,14},{14,12},{16,18},{18,... | collective-permute-start | bytes 3981320 | tf_op jit(solution)/shard_map/ppermute | solution.py:154
  46.3 1.5 fusion.30
  49.3 7.1 %fusion.18 = f32[864,1536]{1,0:T(8,128)S(1)} fusion(bf16[1536,3072]{1,0:T(8,128)(2,1)} %param.11, s32[]{:T(128)S(6)} %select_n.311, bf16[432,1536]{1,0:T(8,128)(2,1)} %collective-permute-done.4, bf16[432,1536]{1,0:T(8,128)(2,1)} %fusion.27), kind=kOutput, calls=%fused_computation.73 | convolution fusion | flops 4082171904 | bytes 12681220 | tf_op jit(solution)/shard_map/dot_general | solution.py:155
  56.4 11.4 %fusion.8 = bf16[864,1536]{1,0:T(8,128)(2,1)S(1)} fusion(f32[864,1536]{1,0:T(8,128)S(1)} %fusion.18, bf16[3072,1536]{1,0:T(8,128)(2,1)} %param.12, s32[]{:T(128)S(6)} %select_n.311, bf16[432,1536]{1,0:T(8,128)(2,1)} %collective-permute-done.3, bf16[432,1536]{1,0:T(8,128)(2,1)} %fusion.30), kind=kOutput, calls=%fused_computation.64 | convolution fusion | flops 4108713984 | bytes 15335428 | tf_op jit(solution)/shard_map/dot_general | solution.py:144
  67.9 2.3 fusion.24
  70.6 8.1 %fusion.1 = bf16[1536,1536]{1,0:T(8,128)(2,1)S(1)} fusion(f32[864,1536]{1,0:T(8,128)} %copy-done.58, bf16[432,1536]{1,0:T(8,128)(2,1)} %collective-permute-done.3, bf16[432,1536]{1,0:T(8,128)(2,1)} %fusion.30), kind=kOutput, calls=%fused_computation.55 | convolution fusion | flops 4098834432 | bytes 12681216 | tf_op jit(solution)/shard_map/dot_general | solution.py:160
  78.8 5.8 %collective-permute-start.25 = (bf16[96,1536]{1,0:T(8,128)(2,1)S(1)}, bf16[96,1536]{1,0:T(8,128)(2,1)S(1)}, u32[]{:S(2)}, u32[]{:S(2)}) collective-permute-start(bf16[96,1536]{1,0:T(8,128)(2,1)S(1)} %get-tuple-element.127), channel_id=1, source_target_pairs={{0,8},{2,10},{8,16},{10,18},{16,24},{18,26},{24,28},{26,30},{28,20... | collective-permute-start | bytes 884744 | tf_op jit(solution)/shard_map/ppermute | solution.py:88
  85.8 7.1 %fusion = bf16[1536,1536]{1,0:T(8,128)(2,1)S(1)} fusion(bf16[864,1536]{1,0:T(8,128)(2,1)S(1)} %fusion.8, bf16[432,1536]{1,0:T(8,128)(2,1)} %collective-permute-done.4, bf16[432,1536]{1,0:T(8,128)(2,1)} %fusion.27), kind=kOutput, calls=%fused_computation.54 | convolution fusion | flops 4086890496 | bytes 10027008 | tf_op jit(solution)/shard_map/dot_general | solution.py:160
  97.3 5.6 %collective-permute-done.10 = bf16[96,1536]{1,0:T(8,128)(2,1)S(1)} collective-permute-done((bf16[96,1536]{1,0:T(8,128)(2,1)S(1)}, bf16[96,1536]{1,0:T(8,128)(2,1)S(1)}, u32[]{:S(2)}, u32[]{:S(2)}) %collective-permute-start.10) | collective-permute-done | bytes 294944 | tf_op jit(solution)/shard_map/ppermute | solution.py:88
  104.0 1.6 collective-permute-start.11
  106.1 3.1 %collective-permute-done.26 = bf16[96,1536]{1,0:T(8,128)(2,1)S(1)} collective-permute-done((bf16[96,1536]{1,0:T(8,128)(2,1)S(1)}, bf16[96,1536]{1,0:T(8,128)(2,1)S(1)}, u32[]{:S(2)}, u32[]{:S(2)}) %collective-permute-start.26) | collective-permute-done | bytes 294944 | tf_op jit(solution)/shard_map/ppermute | solution.py:88
  110.4 1.6 collective-permute-start.27
  112.4 3.1 %collective-permute-done.11 = bf16[96,1536]{1,0:T(8,128)(2,1)S(1)} collective-permute-done((bf16[96,1536]{1,0:T(8,128)(2,1)S(1)}, bf16[96,1536]{1,0:T(8,128)(2,1)S(1)}, u32[]{:S(2)}, u32[]{:S(2)}) %collective-permute-start.11) | collective-permute-done | bytes 294944 | tf_op jit(solution)/shard_map/ppermute | solution.py:88
  116.7 1.6 collective-permute-start.12
  118.8 3.1 %collective-permute-done.27 = bf16[96,1536]{1,0:T(8,128)(2,1)S(1)} collective-permute-done((bf16[96,1536]{1,0:T(8,128)(2,1)S(1)}, bf16[96,1536]{1,0:T(8,128)(2,1)S(1)}, u32[]{:S(2)}, u32[]{:S(2)}) %collective-permute-start.27) | collective-permute-done | bytes 294944 | tf_op jit(solution)/shard_map/ppermute | solution.py:88
  123.0 1.6 collective-permute-start.28
  125.1 3.1 %collective-permute-done.12 = bf16[96,1536]{1,0:T(8,128)(2,1)S(1)} collective-permute-done((bf16[96,1536]{1,0:T(8,128)(2,1)S(1)}, bf16[96,1536]{1,0:T(8,128)(2,1)S(1)}, u32[]{:S(2)}, u32[]{:S(2)}) %collective-permute-start.12) | collective-permute-done | bytes 294944 | tf_op jit(solution)/shard_map/ppermute | solution.py:88
  129.3 1.6 collective-permute-start.13
  131.4 3.1 %collective-permute-done.28 = bf16[96,1536]{1,0:T(8,128)(2,1)S(1)} collective-permute-done((bf16[96,1536]{1,0:T(8,128)(2,1)S(1)}, bf16[96,1536]{1,0:T(8,128)(2,1)S(1)}, u32[]{:S(2)}, u32[]{:S(2)}) %collective-permute-start.28) | collective-permute-done | bytes 294944 | tf_op jit(solution)/shard_map/ppermute | solution.py:88
  135.6 1.6 collective-permute-start.29
  137.7 3.1 %collective-permute-done.13 = bf16[96,1536]{1,0:T(8,128)(2,1)S(1)} collective-permute-done((bf16[96,1536]{1,0:T(8,128)(2,1)S(1)}, bf16[96,1536]{1,0:T(8,128)(2,1)S(1)}, u32[]{:S(2)}, u32[]{:S(2)}) %collective-permute-start.13) | collective-permute-done | bytes 294944 | tf_op jit(solution)/shard_map/ppermute | solution.py:88
  141.9 1.6 collective-permute-start.14
  144.0 2.7 %multiply_reduce_fusion = (f32[432]{0:T(512)S(1)}, f32[432]{0:T(512)S(1)}, f32[432,1536]{1,0:T(8,128)S(1)}) fusion(f32[1536]{0:T(1024)S(1)} %copy-done.53, f32[432]{0:T(512)S(1)} %copy-done.55, f32[432]{0:T(512)S(1)} %copy-done.51, bf16[432,768]{1,0:T(8,128)(2,1)S(1)} %get-tuple-element.143, bf16[432,768]{1,0:T(8,128)(2,1)S(1)} %get-tuple-element.142, ...), kind=kOutput, calls=%fused_computation.94 | convolution fusion | flops 2046393600 | bytes 11369860 | tf_op jit(solution)/shard_map/dot_general | solution.py:166
  146.8 1.6 collective-permute-start.7
  148.4 2.1 collective-permute-done.7
  150.6 1.5 collective-permute-start.6
  153.1 1.6 collective-permute-start.30
  156.1 1.6 collective-permute-start.15
  158.2 5.1 %collective-permute-done.6 = bf16[432,768]{1,0:T(8,128)(2,1)S(1)} collective-permute-done((bf16[432,768]{1,0:T(8,128)(2,1)S(1)}, bf16[432,768]{1,0:T(8,128)(2,1)S(1)}, u32[]{:S(2)}, u32[]{:S(2)}) %collective-permute-start.6) | collective-permute-done | bytes 663584 | tf_op jit(solution)/shard_map/ppermute | solution.py:182
  163.2 1.6 multiply_convert_fusion.2
  164.8 3.2 %fusion.160 = (f32[768]{0:T(1024)S(1)}, f32[768]{0:T(1024)S(1)}, f32[768]{0:T(1024)S(1)}, f32[768]{0:T(1024)S(1)}, f32[768]{0:T(1024)S(1)}, /*index=5*/f32[768]{...) fusion(bf16[3,144,768]{2,1,0:T(8,128)(2,1)S(1)} %bitcast.29, ...), kind=kLoop, calls=%fused_computation.271 | loop fusion | flops 18233856 | bytes 12662784 | tf_op jit(solution)/shard_map/reduce_sum | solution.py:50
  168.1 3.3 %fusion.161 = (f32[768]{0:T(1024)S(1)}, f32[768]{0:T(1024)S(1)}, f32[768]{0:T(1024)S(1)}, f32[768]{0:T(1024)S(1)}, f32[768]{0:T(1024)S(1)}, /*index=5*/f32[768]{...) fusion(bf16[3,144,768]{2,1,0:T(8,128)(2,1)S(1)} %bitcast.30, ...), kind=kLoop, calls=%fused_computation.272 | loop fusion | flops 18233856 | bytes 12662784 | tf_op jit(solution)/shard_map/reduce_sum | solution.py:50
  171.4 2.1 fusion.159
  178.2 1.5 collective-permute-start.41
  181.0 1.6 collective-permute-start.16
  183.1 4.7 %collective-permute-done.41 = bf16[7,7,768]{2,1,0:T(8,128)(2,1)S(1)} collective-permute-done((bf16[7,7,768]{2,1,0:T(8,128)(2,1)S(1)}, bf16[7,7,768]{2,1,0:T(8,128)(2,1)S(1)}, u32[]{:S(2)}, u32[]{:S(2)}) %collective-permute-start.41) | collective-permute-done | bytes 75296 | tf_op jit(solution)/shard_map/ppermute | solution.py:203
  190.4 3.0 %collective-permute-start.42 = (bf16[7,7,768]{2,1,0:T(8,128)(2,1)S(1)}, bf16[7,7,768]{2,1,0:T(8,128)(2,1)S(1)}, u32[]{:S(2)}, u32[]{:S(2)}) collective-permute-start(bf16[7,7,768]{2,1,0:T(8,128)(2,1)S(1)} %add_convert_fusion.30), channel_id=1, source_target_pairs={{0,8},{2,10},{4,12},{6,14},{8,0},{10,2},{12,4},{14,6},{16,24},{18,... | collective-permute-start | bytes 225800 | tf_op jit(solution)/shard_map/ppermute | solution.py:203
  194.7 9.2 %collective-permute-done.42 = bf16[7,7,768]{2,1,0:T(8,128)(2,1)S(1)} collective-permute-done((bf16[7,7,768]{2,1,0:T(8,128)(2,1)S(1)}, bf16[7,7,768]{2,1,0:T(8,128)(2,1)S(1)}, u32[]{:S(2)}, u32[]{:S(2)}) %collective-permute-start.42) | collective-permute-done | bytes 75296 | tf_op jit(solution)/shard_map/ppermute | solution.py:203
  203.9 5.4 %collective-permute-start.43 = (bf16[7,7,768]{2,1,0:T(8,128)(2,1)S(1)}, bf16[7,7,768]{2,1,0:T(8,128)(2,1)S(1)}, u32[]{:S(2)}, u32[]{:S(2)}) collective-permute-start(bf16[7,7,768]{2,1,0:T(8,128)(2,1)S(1)} %add_convert_fusion.29), channel_id=1, source_target_pairs={{0,16},{2,18},{4,20},{6,22},{8,24},{10,26},{12,28},{14,30},{16,0},... | collective-permute-start | bytes 225800 | tf_op jit(solution)/shard_map/ppermute | solution.py:203
  210.9 2.5 %collective-permute-done.43 = bf16[7,7,768]{2,1,0:T(8,128)(2,1)S(1)} collective-permute-done((bf16[7,7,768]{2,1,0:T(8,128)(2,1)S(1)}, bf16[7,7,768]{2,1,0:T(8,128)(2,1)S(1)}, u32[]{:S(2)}, u32[]{:S(2)}) %collective-permute-start.43) | collective-permute-done | bytes 75296 | tf_op jit(solution)/shard_map/ppermute | solution.py:203
  217.9 10.7 %add_convert_fusion = bf16[3,144,768]{2,1,0:T(8,128)(2,1)} fusion(bf16[3,144,768]{2,1,0:T(8,128)(2,1)S(1)} %collective-permute-done.8, bf16[3,144,768]{2,1,0:T(8,128)(2,1)S(1)} %bitcast.35, bf16[3,144,768]{2,1,0:T(8,128)(2,1)S(1)} %collective-permute-done.9, bf16[9,150,768]{2,1,0:T(8,128)(2,1)S(1)} %select_maximum_fusion, f32[768]{0:T(1024)S(1)} %get-tuple-element.106, ...), kind=kLoop, calls=%fused_computation.280 | loop fusion | flops 53415936 | bytes 31337476 | tf_op jit(solution)/shard_map/convert_element_type | solution.py:200
  (285 shorter events, 43.3 us)
Async XLA Ops:
  0.6 8.0 %collective-permute-start = (bf16[3,144,768]{2,1,0:T(8,128)(2,1)}, bf16[3,144,768]{2,1,0:T(8,128)(2,1)S(1)}, u32[]{:S(2)}, u32[]{:S(2)}) collective-permute-start(bf16[3,144,768]{2,1,0:T(8,128)(2,1)} %param.7), channel_id=1, source_target_pairs={{0,2},{2,4},{4,6},{6,8},{8,10},{10,12},{12,14},{14,16},{16,18},{18... | collective-permute-start | bytes 1990664 | tf_op jit(solution)/shard_map/ppermute | solution.py:14
  3.2 6.3 %collective-permute-start.1 = (bf16[3,144,768]{2,1,0:T(8,128)(2,1)}, bf16[3,144,768]{2,1,0:T(8,128)(2,1)S(1)}, u32[]{:S(2)}, u32[]{:S(2)}) collective-permute-start(bf16[3,144,768]{2,1,0:T(8,128)(2,1)} %param.7), channel_id=1, source_target_pairs={{2,0},{4,2},{6,4},{8,6},{10,8},{12,10},{14,12},{16,14},{18,16},{20... | collective-permute-start | bytes 1990664 | tf_op jit(solution)/shard_map/ppermute | solution.py:15
  21.0 11.0 %collective-permute-start.2 = (bf16[432,768]{1,0:T(8,128)(2,1)}, bf16[432,768]{1,0:T(8,128)(2,1)}, u32[]{:S(2)}, u32[]{:S(2)}) collective-permute-start(bf16[432,768]{1,0:T(8,128)(2,1)} %bitcast), channel_id=1, source_target_pairs={{0,1},{1,0},{2,3},{3,2},{4,5},{5,4},{6,7},{7,6},{8,9},{9,8},{10,11... | collective-permute-start | bytes 1990664 | tf_op jit(solution)/shard_map/ppermute | solution.py:134
  35.8 13.5 %collective-permute-start.4 = (bf16[432,1536]{1,0:T(8,128)(2,1)}, bf16[432,1536]{1,0:T(8,128)(2,1)}, u32[]{:S(2)}, u32[]{:S(2)}) collective-permute-start(bf16[432,1536]{1,0:T(8,128)(2,1)} %fusion.27), channel_id=1, source_target_pairs={{0,2},{2,0},{4,6},{6,4},{8,10},{10,8},{12,14},{14,12},{16,18},{18,... | collective-permute-start | bytes 3981320 | tf_op jit(solution)/shard_map/ppermute | solution.py:154
  47.7 8.7 %collective-permute-start.3 = (bf16[432,1536]{1,0:T(8,128)(2,1)}, bf16[432,1536]{1,0:T(8,128)(2,1)}, u32[]{:S(2)}, u32[]{:S(2)}) collective-permute-start(bf16[432,1536]{1,0:T(8,128)(2,1)} %fusion.30), channel_id=1, source_target_pairs={{0,2},{2,0},{4,6},{6,4},{8,10},{10,8},{12,14},{14,12},{16,18},{18,... | collective-permute-start | bytes 3981320 | tf_op jit(solution)/shard_map/ppermute | solution.py:126
  49.3 18.6 %slice-start = ((s8[9437184]{0:T(1024)(128)(4,1)}), s8[4194304]{0:T(1024)(128)(4,1)S(1)}, s32[]{:S(2)}) async-start(s8[9437184]{0:T(1024)(128)(4,1)} %bitcast.42), calls=%async_computation | async-start | bytes 8388608
  49.3 18.6 %slice-start.1 = ((s8[9437184]{0:T(1024)(128)(4,1)}), s8[4194304]{0:T(1024)(128)(4,1)S(1)}, s32[]{:S(2)}) async-start(s8[9437184]{0:T(1024)(128)(4,1)} %bitcast.42), calls=%async_computation.1 | async-start | bytes 8388608
  70.2 73.9 %collective-permute-start.5 = (bf16[432,1536]{1,0:T(8,128)(2,1)S(1)}, bf16[432,1536]{1,0:T(8,128)(2,1)S(1)}, u32[]{:S(2)}, u32[]{:S(2)}) collective-permute-start(bf16[432,1536]{1,0:T(8,128)(2,1)S(1)} %fusion.24), channel_id=1, source_target_pairs={{0,2},{2,0},{4,6},{6,4},{8,10},{10,8},{12,14},{14,12},{16,18},{18,... | collective-permute-start | bytes 3981320 | tf_op jit(solution)/shard_map/ppermute | solution.py:171
  78.7 73.4 %copy-start.11 = (bf16[1536,1536]{1,0:T(8,128)(2,1)}, bf16[1536,1536]{1,0:T(8,128)(2,1)S(1)}, u32[]{:S(2)}) copy-start(bf16[1536,1536]{1,0:T(8,128)(2,1)S(1)} %fusion.1) | copy-start | bytes 14155780
  78.8 16.3 %collective-permute-start.25 = (bf16[96,1536]{1,0:T(8,128)(2,1)S(1)}, bf16[96,1536]{1,0:T(8,128)(2,1)S(1)}, u32[]{:S(2)}, u32[]{:S(2)}) collective-permute-start(bf16[96,1536]{1,0:T(8,128)(2,1)S(1)} %get-tuple-element.127), channel_id=1, source_target_pairs={{0,8},{2,10},{8,16},{10,18},{16,24},{18,26},{24,28},{26,30},{28,20... | collective-permute-start | bytes 884744 | tf_op jit(solution)/shard_map/ppermute | solution.py:88
  84.6 10.4 %collective-permute-start.32 = (bf16[96,1536]{1,0:T(8,128)(2,1)S(1)}, bf16[96,1536]{1,0:T(8,128)(2,1)S(1)}, u32[]{:S(2)}, u32[]{:S(2)}) collective-permute-start(bf16[96,1536]{1,0:T(8,128)(2,1)S(1)} %get-tuple-element.126), channel_id=1, source_target_pairs={{0,4},{2,6},{8,0},{10,2},{16,8},{18,10},{24,16},{26,18},{28,24},{3... | collective-permute-start | bytes 884744 | tf_op jit(solution)/shard_map/ppermute | solution.py:88
  92.9 62.2 %copy-start.10 = (bf16[1536,1536]{1,0:T(8,128)(2,1)}, bf16[1536,1536]{1,0:T(8,128)(2,1)S(1)}, u32[]{:S(2)}) copy-start(bf16[1536,1536]{1,0:T(8,128)(2,1)S(1)} %fusion) | copy-start | bytes 14155780
  93.0 9.9 %collective-permute-start.10 = (bf16[96,1536]{1,0:T(8,128)(2,1)S(1)}, bf16[96,1536]{1,0:T(8,128)(2,1)S(1)}, u32[]{:S(2)}, u32[]{:S(2)}) collective-permute-start(bf16[96,1536]{1,0:T(8,128)(2,1)S(1)} %get-tuple-element.141), channel_id=1, source_target_pairs={{0,8},{2,10},{8,16},{10,18},{16,24},{18,26},{24,28},{26,30},{28,20... | collective-permute-start | bytes 884744 | tf_op jit(solution)/shard_map/ppermute | solution.py:88
  93.9 9.9 %collective-permute-start.17 = (bf16[96,1536]{1,0:T(8,128)(2,1)S(1)}, bf16[96,1536]{1,0:T(8,128)(2,1)S(1)}, u32[]{:S(2)}, u32[]{:S(2)}) collective-permute-start(bf16[96,1536]{1,0:T(8,128)(2,1)S(1)} %get-tuple-element.140), channel_id=1, source_target_pairs={{0,4},{2,6},{8,0},{10,2},{16,8},{18,10},{24,16},{26,18},{28,24},{3... | collective-permute-start | bytes 884744 | tf_op jit(solution)/shard_map/ppermute | solution.py:88
  95.3 14.0 %collective-permute-start.26 = (bf16[96,1536]{1,0:T(8,128)(2,1)S(1)}, bf16[96,1536]{1,0:T(8,128)(2,1)S(1)}, u32[]{:S(2)}, u32[]{:S(2)}) collective-permute-start(bf16[96,1536]{1,0:T(8,128)(2,1)S(1)} %get-tuple-element.125), channel_id=1, source_target_pairs={{0,8},{2,10},{8,16},{10,18},{16,24},{18,26},{24,28},{26,30},{28,20... | collective-permute-start | bytes 884744 | tf_op jit(solution)/shard_map/ppermute | solution.py:88
  96.2 14.0 %collective-permute-start.33 = (bf16[96,1536]{1,0:T(8,128)(2,1)S(1)}, bf16[96,1536]{1,0:T(8,128)(2,1)S(1)}, u32[]{:S(2)}, u32[]{:S(2)}) collective-permute-start(bf16[96,1536]{1,0:T(8,128)(2,1)S(1)} %get-tuple-element.124), channel_id=1, source_target_pairs={{0,4},{2,6},{8,0},{10,2},{16,8},{18,10},{24,16},{26,18},{28,24},{3... | collective-permute-start | bytes 884744 | tf_op jit(solution)/shard_map/ppermute | solution.py:88
  104.0 11.5 %collective-permute-start.11 = (bf16[96,1536]{1,0:T(8,128)(2,1)S(1)}, bf16[96,1536]{1,0:T(8,128)(2,1)S(1)}, u32[]{:S(2)}, u32[]{:S(2)}) collective-permute-start(bf16[96,1536]{1,0:T(8,128)(2,1)S(1)} %get-tuple-element.139), channel_id=1, source_target_pairs={{0,8},{2,10},{8,16},{10,18},{16,24},{18,26},{24,28},{26,30},{28,20... | collective-permute-start | bytes 884744 | tf_op jit(solution)/shard_map/ppermute | solution.py:88
  105.7 10.8 %collective-permute-start.18 = (bf16[96,1536]{1,0:T(8,128)(2,1)S(1)}, bf16[96,1536]{1,0:T(8,128)(2,1)S(1)}, u32[]{:S(2)}, u32[]{:S(2)}) collective-permute-start(bf16[96,1536]{1,0:T(8,128)(2,1)S(1)} %get-tuple-element.138), channel_id=1, source_target_pairs={{0,4},{2,6},{8,0},{10,2},{16,8},{18,10},{24,16},{26,18},{28,24},{3... | collective-permute-start | bytes 884744 | tf_op jit(solution)/shard_map/ppermute | solution.py:88
  110.4 11.5 %collective-permute-start.27 = (bf16[96,1536]{1,0:T(8,128)(2,1)S(1)}, bf16[96,1536]{1,0:T(8,128)(2,1)S(1)}, u32[]{:S(2)}, u32[]{:S(2)}) collective-permute-start(bf16[96,1536]{1,0:T(8,128)(2,1)S(1)} %get-tuple-element.123), channel_id=1, source_target_pairs={{0,8},{2,10},{8,16},{10,18},{16,24},{18,26},{24,28},{26,30},{28,20... | collective-permute-start | bytes 884744 | tf_op jit(solution)/shard_map/ppermute | solution.py:88
  112.0 10.8 %collective-permute-start.34 = (bf16[96,1536]{1,0:T(8,128)(2,1)S(1)}, bf16[96,1536]{1,0:T(8,128)(2,1)S(1)}, u32[]{:S(2)}, u32[]{:S(2)}) collective-permute-start(bf16[96,1536]{1,0:T(8,128)(2,1)S(1)} %get-tuple-element.122), channel_id=1, source_target_pairs={{0,4},{2,6},{8,0},{10,2},{16,8},{18,10},{24,16},{26,18},{28,24},{3... | collective-permute-start | bytes 884744 | tf_op jit(solution)/shard_map/ppermute | solution.py:88
  116.7 11.5 %collective-permute-start.12 = (bf16[96,1536]{1,0:T(8,128)(2,1)S(1)}, bf16[96,1536]{1,0:T(8,128)(2,1)S(1)}, u32[]{:S(2)}, u32[]{:S(2)}) collective-permute-start(bf16[96,1536]{1,0:T(8,128)(2,1)S(1)} %get-tuple-element.137), channel_id=1, source_target_pairs={{0,8},{2,10},{8,16},{10,18},{16,24},{18,26},{24,28},{26,30},{28,20... | collective-permute-start | bytes 884744 | tf_op jit(solution)/shard_map/ppermute | solution.py:88
  118.3 10.8 %collective-permute-start.19 = (bf16[96,1536]{1,0:T(8,128)(2,1)S(1)}, bf16[96,1536]{1,0:T(8,128)(2,1)S(1)}, u32[]{:S(2)}, u32[]{:S(2)}) collective-permute-start(bf16[96,1536]{1,0:T(8,128)(2,1)S(1)} %get-tuple-element.136), channel_id=1, source_target_pairs={{0,4},{2,6},{8,0},{10,2},{16,8},{18,10},{24,16},{26,18},{28,24},{3... | collective-permute-start | bytes 884744 | tf_op jit(solution)/shard_map/ppermute | solution.py:88
  123.0 11.5 %collective-permute-start.28 = (bf16[96,1536]{1,0:T(8,128)(2,1)S(1)}, bf16[96,1536]{1,0:T(8,128)(2,1)S(1)}, u32[]{:S(2)}, u32[]{:S(2)}) collective-permute-start(bf16[96,1536]{1,0:T(8,128)(2,1)S(1)} %get-tuple-element.121), channel_id=1, source_target_pairs={{0,8},{2,10},{8,16},{10,18},{16,24},{18,26},{24,28},{26,30},{28,20... | collective-permute-start | bytes 884744 | tf_op jit(solution)/shard_map/ppermute | solution.py:88
  124.6 10.8 %collective-permute-start.35 = (bf16[96,1536]{1,0:T(8,128)(2,1)S(1)}, bf16[96,1536]{1,0:T(8,128)(2,1)S(1)}, u32[]{:S(2)}, u32[]{:S(2)}) collective-permute-start(bf16[96,1536]{1,0:T(8,128)(2,1)S(1)} %get-tuple-element.120), channel_id=1, source_target_pairs={{0,4},{2,6},{8,0},{10,2},{16,8},{18,10},{24,16},{26,18},{28,24},{3... | collective-permute-start | bytes 884744 | tf_op jit(solution)/shard_map/ppermute | solution.py:88
  129.3 11.5 %collective-permute-start.13 = (bf16[96,1536]{1,0:T(8,128)(2,1)S(1)}, bf16[96,1536]{1,0:T(8,128)(2,1)S(1)}, u32[]{:S(2)}, u32[]{:S(2)}) collective-permute-start(bf16[96,1536]{1,0:T(8,128)(2,1)S(1)} %get-tuple-element.135), channel_id=1, source_target_pairs={{0,8},{2,10},{8,16},{10,18},{16,24},{18,26},{24,28},{26,30},{28,20... | collective-permute-start | bytes 884744 | tf_op jit(solution)/shard_map/ppermute | solution.py:88
  130.9 10.8 %collective-permute-start.20 = (bf16[96,1536]{1,0:T(8,128)(2,1)S(1)}, bf16[96,1536]{1,0:T(8,128)(2,1)S(1)}, u32[]{:S(2)}, u32[]{:S(2)}) collective-permute-start(bf16[96,1536]{1,0:T(8,128)(2,1)S(1)} %get-tuple-element.134), channel_id=1, source_target_pairs={{0,4},{2,6},{8,0},{10,2},{16,8},{18,10},{24,16},{26,18},{28,24},{3... | collective-permute-start | bytes 884744 | tf_op jit(solution)/shard_map/ppermute | solution.py:88
  135.6 16.4 %collective-permute-start.29 = (bf16[96,1536]{1,0:T(8,128)(2,1)S(1)}, bf16[96,1536]{1,0:T(8,128)(2,1)S(1)}, u32[]{:S(2)}, u32[]{:S(2)}) collective-permute-start(bf16[96,1536]{1,0:T(8,128)(2,1)S(1)} %get-tuple-element.119), channel_id=1, source_target_pairs={{0,8},{2,10},{8,16},{10,18},{16,24},{18,26},{24,28},{26,30},{28,20... | collective-permute-start | bytes 884744 | tf_op jit(solution)/shard_map/ppermute | solution.py:88
  137.3 14.8 %collective-permute-start.36 = (bf16[96,1536]{1,0:T(8,128)(2,1)S(1)}, bf16[96,1536]{1,0:T(8,128)(2,1)S(1)}, u32[]{:S(2)}, u32[]{:S(2)}) collective-permute-start(bf16[96,1536]{1,0:T(8,128)(2,1)S(1)} %get-tuple-element.118), channel_id=1, source_target_pairs={{0,4},{2,6},{8,0},{10,2},{16,8},{18,10},{24,16},{26,18},{28,24},{3... | collective-permute-start | bytes 884744 | tf_op jit(solution)/shard_map/ppermute | solution.py:88
  141.9 13.2 %collective-permute-start.14 = (bf16[96,1536]{1,0:T(8,128)(2,1)S(1)}, bf16[96,1536]{1,0:T(8,128)(2,1)S(1)}, u32[]{:S(2)}, u32[]{:S(2)}) collective-permute-start(bf16[96,1536]{1,0:T(8,128)(2,1)S(1)} %get-tuple-element.133), channel_id=1, source_target_pairs={{0,8},{2,10},{8,16},{10,18},{16,24},{18,26},{24,28},{26,30},{28,20... | collective-permute-start | bytes 884744 | tf_op jit(solution)/shard_map/ppermute | solution.py:88
  143.6 11.6 %collective-permute-start.21 = (bf16[96,1536]{1,0:T(8,128)(2,1)S(1)}, bf16[96,1536]{1,0:T(8,128)(2,1)S(1)}, u32[]{:S(2)}, u32[]{:S(2)}) collective-permute-start(bf16[96,1536]{1,0:T(8,128)(2,1)S(1)} %get-tuple-element.132), channel_id=1, source_target_pairs={{0,4},{2,6},{8,0},{10,2},{16,8},{18,10},{24,16},{26,18},{28,24},{3... | collective-permute-start | bytes 884744 | tf_op jit(solution)/shard_map/ppermute | solution.py:88
  146.8 3.8 %collective-permute-start.7 = (f32[2,432]{1,0:T(2,128)S(1)}, f32[2,432]{1,0:T(2,128)S(1)}, u32[]{:S(2)}, u32[]{:S(2)}) collective-permute-start(f32[2,432]{1,0:T(2,128)S(1)} %pad_maximum_fusion.9), channel_id=1, source_target_pairs={{0,1},{1,0},{2,3},{3,2},{4,5},{5,4},{6,7},{7,6},{8,9},{9,8},{10,11... | collective-permute-start | bytes 10376 | tf_op jit(solution)/shard_map/ppermute | solution.py:184
  150.6 12.7 %collective-permute-start.6 = (bf16[432,768]{1,0:T(8,128)(2,1)S(1)}, bf16[432,768]{1,0:T(8,128)(2,1)S(1)}, u32[]{:S(2)}, u32[]{:S(2)}) collective-permute-start(bf16[432,768]{1,0:T(8,128)(2,1)S(1)} %dynamic-slice_convert_fusion), channel_id=1, source_target_pairs={{0,1},{1,0},{2,3},{3,2},{4,5},{5,4},{6,7},{7,6},{8,9},{9,8},{10,11... | collective-permute-start | bytes 1990664 | tf_op jit(solution)/shard_map/ppermute | solution.py:182
  153.1 21.5 %collective-permute-start.30 = (bf16[96,1536]{1,0:T(8,128)(2,1)}, bf16[96,1536]{1,0:T(8,128)(2,1)}, u32[]{:S(2)}, u32[]{:S(2)}) collective-permute-start(bf16[96,1536]{1,0:T(8,128)(2,1)} %get-tuple-element.117), channel_id=1, source_target_pairs={{0,8},{2,10},{8,16},{10,18},{16,24},{18,26},{24,28},{26,30},{28,20... | collective-permute-start | bytes 884744 | tf_op jit(solution)/shard_map/ppermute | solution.py:88
  154.7 19.9 %collective-permute-start.37 = (bf16[96,1536]{1,0:T(8,128)(2,1)}, bf16[96,1536]{1,0:T(8,128)(2,1)}, u32[]{:S(2)}, u32[]{:S(2)}) collective-permute-start(bf16[96,1536]{1,0:T(8,128)(2,1)} %get-tuple-element.116), channel_id=1, source_target_pairs={{0,4},{2,6},{8,0},{10,2},{16,8},{18,10},{24,16},{26,18},{28,24},{3... | collective-permute-start | bytes 884744 | tf_op jit(solution)/shard_map/ppermute | solution.py:88
  156.1 23.5 %collective-permute-start.15 = (bf16[96,1536]{1,0:T(8,128)(2,1)}, bf16[96,1536]{1,0:T(8,128)(2,1)}, u32[]{:S(2)}, u32[]{:S(2)}) collective-permute-start(bf16[96,1536]{1,0:T(8,128)(2,1)} %get-tuple-element.131), channel_id=1, source_target_pairs={{0,8},{2,10},{8,16},{10,18},{16,24},{18,26},{24,28},{26,30},{28,20... | collective-permute-start | bytes 884744 | tf_op jit(solution)/shard_map/ppermute | solution.py:88
  157.8 21.9 %collective-permute-start.22 = (bf16[96,1536]{1,0:T(8,128)(2,1)}, bf16[96,1536]{1,0:T(8,128)(2,1)}, u32[]{:S(2)}, u32[]{:S(2)}) collective-permute-start(bf16[96,1536]{1,0:T(8,128)(2,1)} %get-tuple-element.130), channel_id=1, source_target_pairs={{0,4},{2,6},{8,0},{10,2},{16,8},{18,10},{24,16},{26,18},{28,24},{3... | collective-permute-start | bytes 884744 | tf_op jit(solution)/shard_map/ppermute | solution.py:88
  174.6 3.6 %collective-permute-start.40 = (bf16[7,7,768]{2,1,0:T(8,128)(2,1)S(1)}, bf16[7,7,768]{2,1,0:T(8,128)(2,1)S(1)}, u32[]{:S(2)}, u32[]{:S(2)}) collective-permute-start(bf16[7,7,768]{2,1,0:T(8,128)(2,1)S(1)} %multiply_convert_fusion.3), channel_id=1, source_target_pairs={{0,2},{2,0},{4,6},{6,4},{8,10},{10,8},{12,14},{14,12},{16,18},{18,... | collective-permute-start | bytes 225800 | tf_op jit(solution)/shard_map/ppermute | solution.py:203
  176.1 13.1 %collective-permute-start.31 = (bf16[96,1536]{1,0:T(8,128)(2,1)S(1)}, bf16[96,1536]{1,0:T(8,128)(2,1)S(1)}, u32[]{:S(2)}, u32[]{:S(2)}) collective-permute-start(bf16[96,1536]{1,0:T(8,128)(2,1)S(1)} %get-tuple-element.115), channel_id=1, source_target_pairs={{0,8},{2,10},{8,16},{10,18},{16,24},{18,26},{24,28},{26,30},{28,20... | collective-permute-start | bytes 884744 | tf_op jit(solution)/shard_map/ppermute | solution.py:88
  177.2 13.3 %collective-permute-start.38 = (bf16[96,1536]{1,0:T(8,128)(2,1)S(1)}, bf16[96,1536]{1,0:T(8,128)(2,1)S(1)}, u32[]{:S(2)}, u32[]{:S(2)}) collective-permute-start(bf16[96,1536]{1,0:T(8,128)(2,1)S(1)} %get-tuple-element.114), channel_id=1, source_target_pairs={{0,4},{2,6},{8,0},{10,2},{16,8},{18,10},{24,16},{26,18},{28,24},{3... | collective-permute-start | bytes 884744 | tf_op jit(solution)/shard_map/ppermute | solution.py:88
  178.2 9.6 %collective-permute-start.41 = (bf16[7,7,768]{2,1,0:T(8,128)(2,1)S(1)}, bf16[7,7,768]{2,1,0:T(8,128)(2,1)S(1)}, u32[]{:S(2)}, u32[]{:S(2)}) collective-permute-start(bf16[7,7,768]{2,1,0:T(8,128)(2,1)S(1)} %add_convert_fusion.31), channel_id=1, source_target_pairs={{0,4},{2,6},{4,0},{6,2},{8,12},{10,14},{12,8},{14,10},{16,20},{18,... | collective-permute-start | bytes 225800 | tf_op jit(solution)/shard_map/ppermute | solution.py:203
  181.0 22.9 %collective-permute-start.16 = (bf16[96,1536]{1,0:T(8,128)(2,1)S(1)}, bf16[96,1536]{1,0:T(8,128)(2,1)S(1)}, u32[]{:S(2)}, u32[]{:S(2)}) collective-permute-start(bf16[96,1536]{1,0:T(8,128)(2,1)S(1)} %get-tuple-element.129), channel_id=1, source_target_pairs={{0,8},{2,10},{8,16},{10,18},{16,24},{18,26},{24,28},{26,30},{28,20... | collective-permute-start | bytes 884744 | tf_op jit(solution)/shard_map/ppermute | solution.py:88
  182.6 26.7 %collective-permute-start.23 = (bf16[96,1536]{1,0:T(8,128)(2,1)S(1)}, bf16[96,1536]{1,0:T(8,128)(2,1)S(1)}, u32[]{:S(2)}, u32[]{:S(2)}) collective-permute-start(bf16[96,1536]{1,0:T(8,128)(2,1)S(1)} %get-tuple-element.128), channel_id=1, source_target_pairs={{0,4},{2,6},{8,0},{10,2},{16,8},{18,10},{24,16},{26,18},{28,24},{3... | collective-permute-start | bytes 884744 | tf_op jit(solution)/shard_map/ppermute | solution.py:88
  187.8 28.9 %collective-permute-start.8 = (bf16[3,144,768]{2,1,0:T(8,128)(2,1)S(1)}, bf16[3,144,768]{2,1,0:T(8,128)(2,1)S(1)}, u32[]{:S(2)}, u32[]{:S(2)}) collective-permute-start(bf16[3,144,768]{2,1,0:T(8,128)(2,1)S(1)} %bitcast.32), channel_id=1, source_target_pairs={{0,2},{2,4},{4,6},{6,8},{8,10},{10,12},{12,14},{14,16},{16,18},{18... | collective-permute-start | bytes 1990664 | tf_op jit(solution)/shard_map/ppermute | solution.py:14
  189.1 27.5 %collective-permute-start.9 = (bf16[3,144,768]{2,1,0:T(8,128)(2,1)S(1)}, bf16[3,144,768]{2,1,0:T(8,128)(2,1)S(1)}, u32[]{:S(2)}, u32[]{:S(2)}) collective-permute-start(bf16[3,144,768]{2,1,0:T(8,128)(2,1)S(1)} %bitcast.33), channel_id=1, source_target_pairs={{2,0},{4,2},{6,4},{8,6},{10,8},{12,10},{14,12},{16,14},{18,16},{20... | collective-permute-start | bytes 1990664 | tf_op jit(solution)/shard_map/ppermute | solution.py:15
  190.4 13.5 %collective-permute-start.42 = (bf16[7,7,768]{2,1,0:T(8,128)(2,1)S(1)}, bf16[7,7,768]{2,1,0:T(8,128)(2,1)S(1)}, u32[]{:S(2)}, u32[]{:S(2)}) collective-permute-start(bf16[7,7,768]{2,1,0:T(8,128)(2,1)S(1)} %add_convert_fusion.30), channel_id=1, source_target_pairs={{0,8},{2,10},{4,12},{6,14},{8,0},{10,2},{12,4},{14,6},{16,24},{18,... | collective-permute-start | bytes 225800 | tf_op jit(solution)/shard_map/ppermute | solution.py:203
  203.9 10.2 %collective-permute-start.39 = (bf16[96,1536]{1,0:T(8,128)(2,1)S(1)}, bf16[96,1536]{1,0:T(8,128)(2,1)S(1)}, u32[]{:S(2)}, u32[]{:S(2)}) collective-permute-start(bf16[96,1536]{1,0:T(8,128)(2,1)S(1)} %get-tuple-element.108), channel_id=1, source_target_pairs={{0,2},{2,0},{4,6},{6,4},{8,10},{10,8},{12,14},{14,12},{16,18},{18,... | collective-permute-start | bytes 884744 | tf_op jit(solution)/shard_map/ppermute | solution.py:98
  203.9 9.5 %collective-permute-start.43 = (bf16[7,7,768]{2,1,0:T(8,128)(2,1)S(1)}, bf16[7,7,768]{2,1,0:T(8,128)(2,1)S(1)}, u32[]{:S(2)}, u32[]{:S(2)}) collective-permute-start(bf16[7,7,768]{2,1,0:T(8,128)(2,1)S(1)} %add_convert_fusion.29), channel_id=1, source_target_pairs={{0,16},{2,18},{4,20},{6,22},{8,24},{10,26},{12,28},{14,30},{16,0},... | collective-permute-start | bytes 225800 | tf_op jit(solution)/shard_map/ppermute | solution.py:203
  210.6 3.6 %collective-permute-start.24 = (bf16[96,1536]{1,0:T(8,128)(2,1)S(1)}, bf16[96,1536]{1,0:T(8,128)(2,1)S(1)}, u32[]{:S(2)}, u32[]{:S(2)}) collective-permute-start(bf16[96,1536]{1,0:T(8,128)(2,1)S(1)} %get-tuple-element.111), channel_id=1, source_target_pairs={{0,2},{2,0},{4,6},{6,4},{8,10},{10,8},{12,14},{14,12},{16,18},{18,... | collective-permute-start | bytes 884744 | tf_op jit(solution)/shard_map/ppermute | solution.py:98
  (58 other events, 184.1 us)

commit v2 on v1

--- a/solution.py
+++ b/solution.py
@@ -13,7 +13,7 @@
     tail = cells[cells.shape[0] - width :]
     above = lax.ppermute(tail, "rows", [(i, i + 1) for i in range(ends)])
     below = lax.ppermute(head, "rows", [(i + 1, i) for i in range(ends)])
-    return jnp.concatenate([above, cells, below], axis=0)
+    return above, below
 
 
 def conv_taps(padded, kernel, height, width):
@@ -38,10 +38,10 @@
     return result
 
 
-def kernel_terms(grad_conv, padded, height, width):
+def kernel_terms(grad_conv, padded, height, width, tap_rows):
     grad_float = grad_conv.astype(jnp.float32)
     rows_list = []
-    for tap_row in range(7):
+    for tap_row in tap_rows:
         cols_list = []
         for tap_col in range(7):
             window = padded[tap_row : tap_row + height, tap_col : tap_col + width].astype(
@@ -56,43 +56,20 @@
     return jax.nn.gelu(value, approximate=True)
 
 
-def chip_at(place, chips):
-    place = place % chips
-    half = chips // 2
-    return jnp.where(place < half, 2 * place, 2 * (chips - 1 - place) + 1)
-
-
-def ring_pairs(chips, step):
-    def chip(place):
-        place = place % chips
-        half = chips // 2
-        return 2 * place if place < half else 2 * (chips - 1 - place) + 1
-
-    return [
-        (2 * chip(p) + core, 2 * chip(p + step) + core) for p in range(chips) for core in range(2)
-    ]
-
-
-def ring_sums(part, place, chips):
-    share = part.shape[0] // chips
-    half = share // 2
-
-    def piece(position, side):
-        return lax.dynamic_slice_in_dim(
-            part, chip_at(position, chips) * share + side * half, half, 0
-        )
-
-    sums = [piece(place + chips - 1, 0), piece(place + 1, 1)]
-    for step in range(chips - 1):
-        for side, way in ((0, 1), (1, -1)):
-            got = lax.ppermute(sums[side], "rows", ring_pairs(chips, way))
-            own = piece(place + 2 * chips - way * (2 + step), side)
-            total = got.astype(jnp.float32) + own.astype(jnp.float32)
-            sums[side] = total.astype(jnp.bfloat16)
-    return sums
-
-
-def own_rows(sums, core, swap):
+def tie(value, *first):
+    return lax.optimization_barrier((value, first))[0]
+
+
+def chip_sums(part, chips):
+    groups = [[2 * chip + core for chip in range(chips)] for core in range(2)]
+    return lax.psum_scatter(
+        part, "rows", scatter_dimension=0, axis_index_groups=groups, tiled=True
+    )
+
+
+def own_rows(total, core, swap):
+    half = total.shape[0] // 2
+    sums = (total[:half], total[half:])
     mine = jnp.where(core == 0, sums[0], sums[1])
     theirs = jnp.where(core == 0, sums[1], sums[0])
     got = lax.ppermute(theirs, "rows", swap)
@@ -110,28 +87,40 @@
     chips = rows // 2
     me = lax.axis_index("rows")
     lane = lax.axis_index("chan")
-    core = me % 2
-    chip = me // 2
-    place = jnp.where(chip % 2 == 0, chip // 2, chips - 1 - chip // 2)
+    core = lax.rem(me, 2)
     swap = [(i, i ^ 1) for i in range(rows)]
     cross = [(0, 1), (1, 0)]
     scale = 1.0 / math.sqrt(height * rows * width)
     offset = lane * local_ch
     units = w_in.shape[1] // 2
 
-    rimmed = halo(feature, 3)
+    above, below = halo(feature, 3)
     grad_mixed = (cotangent.reshape(pixels, channels).astype(jnp.float32) * layer_scale).astype(
         jnp.bfloat16
     )
     mixed_both = jnp.concatenate([grad_mixed, lax.ppermute(grad_mixed, "rows", swap)], axis=0)
     in_part = lax.dynamic_slice_in_dim(w_in, core * units, units, 1)
     out_part = lax.dynamic_slice_in_dim(w_out, core * units, units, 0)
+    grad_activ = lax.dot_general(
+        mixed_both, out_part, (((1,), (1,)), ((), ())), preferred_element_type=jnp.float32
+    )
+    above, below = tie((above, below), mixed_both, out_part, in_part)
+    rimmed = jnp.concatenate([above, feature, below], axis=0)
 
     padded = jnp.pad(rimmed, ((0, 0), (3, 3), (0, 0)))
-    conv_local = conv_taps(padded, kernel, height, width).astype(jnp.bfloat16)
-    conv_local = conv_local.reshape(pixels, local_ch)
+    lines = []
+    passed = []
+    for line in range(height):
+        done = conv_taps(padded[line : line + 7], kernel, 1, width).astype(jnp.bfloat16)
+        done = done.reshape(width, local_ch)
+        if lines:
+            done = tie(done, lines[-1])
+        lines.append(done)
+        if chan == 2:
+            passed.append(lax.ppermute(done, "chan", cross))
+    conv_local = jnp.concatenate(lines, axis=0)
     if chan == 2:
-        conv_other = lax.ppermute(conv_local, "chan", cross)
+        conv_other = jnp.concatenate(tie(passed, grad_activ), axis=0)
         conv_full = jnp.concatenate(
             [
                 jnp.where(lane == 0, conv_local, conv_other),
@@ -141,9 +130,6 @@
         )
     else:
         conv_full = lax.all_gather(conv_local, "chan", axis=1, tiled=True)
-    grad_activ = lax.dot_general(
-        mixed_both, out_part, (((1,), (1,)), ((), ())), preferred_element_type=jnp.float32
-    )
     values = conv_full.astype(jnp.float32)
     mean = jnp.mean(values, axis=1, keepdims=True)
     centred = values - mean
@@ -167,10 +153,10 @@
             grads, in_part, (((1,), (1,)), ((), ())), preferred_element_type=jnp.float32
         )
 
-    out_sums = ring_sums(pixel_sum(mixed_both, activ), place, chips)
+    out_sum = chip_sums(pixel_sum(mixed_both, activ), chips)
     back_other = lax.ppermute(back(grad_hidden[pixels:]).astype(jnp.bfloat16), "rows", swap)
+    in_sum = chip_sums(pixel_sum(normed_both, grad_hidden), chips)
     back_own = back(grad_hidden[:pixels]) + back_other.astype(jnp.float32)
-    in_sums = ring_sums(pixel_sum(normed_both, grad_hidden), place, chips)
 
     scaled_part = back_own * ln_gain
     first_part = jnp.sum(scaled_part, axis=1)
@@ -193,19 +179,31 @@
     scaled = grad_normed * lax.dynamic_slice_in_dim(ln_gain, offset, local_ch, 0)
     grad_local = rstd * (scaled - first_mean - nhat_own * second_mean)
     grad_conv = grad_local.astype(jnp.bfloat16).reshape(height, width, local_ch)
-    grad_rimmed = halo(grad_conv, 3)
-    kernel_sum = (kernel_terms(grad_conv, padded, height, width) * scale).astype(jnp.bfloat16)
+    grad_above, grad_below = halo(grad_conv, 3)
+    grad_rimmed = jnp.concatenate([grad_above, grad_conv, grad_below], axis=0)
     grad_pad = jnp.pad(grad_rimmed, ((0, 0), (3, 3), (0, 0)))
     cot_own = lax.dynamic_slice_in_dim(cotangent, offset, local_ch, 2).astype(jnp.float32)
-    grad_feature = (cot_own + conv_back(grad_pad, kernel, height, width)).astype(jnp.bfloat16)
+
+    def terms(grads, tap_rows):
+        return (kernel_terms(grads, padded, height, width, tap_rows) * scale).astype(
+            jnp.bfloat16
+        )
+
+    def feature_line(line, grads):
+        back_line = conv_back(grads, kernel, 1, width)
+        return (cot_own[line : line + 1] + back_line).astype(jnp.bfloat16)
+
+    kernel_sum = terms(grad_conv, range(7))
+    lines = [feature_line(line, grad_pad[line : line + 7]) for line in range(height)]
+    grad_feature = jnp.concatenate(lines, axis=0)
     span = 1
     while span < rows:
         other = lax.ppermute(kernel_sum, "rows", [(i, i ^ span) for i in range(rows)])
         total = kernel_sum.astype(jnp.float32) + other.astype(jnp.float32)
         span *= 2
         kernel_sum = total if span >= rows else total.astype(jnp.bfloat16)
-    grad_w_out = own_rows(out_sums, core, swap).T
-    grad_w_in = own_rows(in_sums, core, swap)
+    grad_w_out = own_rows(out_sum, core, swap).T
+    grad_w_in = own_rows(in_sum, core, swap)
     return (grad_feature, grad_w_in, grad_w_out, kernel_sum)
 
 

time: 229 us -> 288 us (1.26)
  waiting for transfers between devices: 64.4 us -> 141 us
  starting transfers between devices: 66.6 us -> 25.4 us
  between operations: 2.33 us -> 15.7 us
  local copies, waits for them, and re-layouts: 6.94 us -> 14.4 us
  matrix products: 38.7 us -> 43.3 us
    reduce_scatter x0 -> x2, waiting for transfers between devices: none -> 113 us  [chip_sums(): lax.psum_scatter(part, 'rows', scatter_dimension=0, axis_index_groups=gro...]
    ppermute x29 -> x3, waiting for transfers between devices: 40 us -> 1.96 us  [shards(): passed.append(lax.ppermute(done, 'chan', cross))]
    ppermute x29 -> x3, starting transfers between devices: 35.8 us -> 3.74 us  [shards(): passed.append(lax.ppermute(done, 'chan', cross))]
    convert_element_type x15 -> x5, other arithmetic: 27.2 us -> 10.8 us  [the longest x3 9.54 us: feature_line(): return (cot_own[line:line + 1] + back_line).astype(jnp.bfloat16)]
    ppermute x1, starting transfers between devices: 10.5 us -> 0.12 us  [shards(): lax.ppermute(normed, 'rows', swap)]
    reshape x0 -> x3, other arithmetic: none -> 9.03 us  [shards(): done = done.reshape(width, local_ch)]
    dot_general x2, matrix products: 5 us -> 12.1 us  [back(): lax.dot_general(grads, in_part, (((1,), (1,)), ((), ())), preferred_eleme...]
    dynamic_slice x2 -> x1, local copies, waits for them, and re-layouts: 0.1 us -> 6.56 us  [shards(): in_part = lax.dynamic_slice_in_dim(w_in, core * units, units, 1)]
  transfers between devices with their start and end apart: 44 -> 20, of which waited for: 22 -> 10; matrix products, arithmetic and copies ran while one was open for 24% -> 28% of each run, Pallas kernels for 0% -> 0%
where the time goes in v2:
time: 288 us
  waiting for transfers between devices  141 us (49%)
  other arithmetic  47.3 us (16%)
  matrix products  43.3 us (15%)
  starting transfers between devices  25.4 us (9%)
  between operations  15.7 us (5%)
  local copies, waits for them, and re-layouts  14.4 us (5%)
    reduce_scatter x2, waiting for transfers between devices, chip_sums(): lax.psum_scatter(part, 'rows', scatter_dimension=0, axis_index_groups=gro...  113 us
    dot_general x2, matrix products, pixel_sum(): lax.dot_general(left, right, (((0,), (0,)), ((), ())), preferred_element_...  16 us
    ppermute x4, waiting for transfers between devices, shards(): lax.ppermute(kernel_sum, 'rows', [(i, i ^ span) for i in range(rows)])  14.5 us
    dot_general x2, matrix products, back(): lax.dot_general(grads, in_part, (((1,), (1,)), ((), ())), preferred_eleme...  12.1 us
    reduce_sum x3, other arithmetic, kernel_terms(): cols_list.append(jnp.sum(grad_float * window, axis=(0, 1)))  9.73 us
    convert_element_type x3, other arithmetic, feature_line(): return (cot_own[line:line + 1] + back_line).astype(jnp.bfloat16)  9.54 us
    ppermute x4, starting transfers between devices, shards(): lax.ppermute(kernel_sum, 'rows', [(i, i ^ span) for i in range(rows)])  9.51 us
    dot_general x1, matrix products, shards(): hidden = jnp.dot(normed_both, in_part, preferred_element_type=jnp.float32)  9.16 us
  transfers between devices with their start and end apart: 20, of which 10 were waited for; matrix products, arithmetic and copies ran while one was open for 28% of the time, Pallas kernels for 0%

profile of v2, /device:TPU:0, one launch (start us, length us, event | category | flops | bytes accessed | tf_op | source)
XLA Modules:
  0.0 287.5 jit_solution(6804084594119430392)
XLA Ops:
  7.2 2.5 collective-permute-start
  9.8 1.3 collective-permute-start.1
  11.1 2.6 fusion.17
  13.7 3.2 %collective-permute-start.2 = (bf16[432,1536]{1,0:T(8,128)(2,1)}, bf16[432,1536]{1,0:T(8,128)(2,1)}, u32[]{:S(2)}, u32[]{:S(2)}) collective-permute-start(bf16[432,1536]{1,0:T(8,128)(2,1)} %fusion.17), channel_id=1, source_target_pairs={{0,2},{2,0},{4,6},{6,4},{8,10},{10,8},{12,14},{14,12},{16,18},{18,... | collective-permute-start | bytes 3981320 | tf_op jit(solution)/shard_map/ppermute | solution.py:101
  18.5 6.6 %constant_dynamic-slice_fusion = (bf16[1536,1536]{1,0:T(8,128)(2,1)S(1)}, bf16[1536,1536]{1,0:T(8,128)(2,1)}) fusion(bf16[1536,3072]{1,0:T(8,128)(2,1)} %param.11, s32[]{:T(128)S(6)} %select_n.62, bf16[3072,1536]{1,0:T(8,128)(2,1)} %param.12), kind=kLoop, calls=%fused_computation.799 | loop fusion | bytes 18874372 | tf_op jit(solution)/shard_map/dynamic_slice | solution.py:102
  26.1 2.7 fusion.26
  29.1 3.1 %fusion.378 = bf16[144,768]{1,0:T(8,128)(2,1)S(1)} fusion(f32[768]{0:T(1024)S(1)} %copy-done.55, f32[768]{0:T(1024)S(1)} %copy-done.57, f32[768]{0:T(1024)S(1)} %get-tuple-element.74, f32[768]{0:T(1024)S(1)} %get-tuple-element.75, f32[768]{0:T(1024)S(1)} %get-tuple-element.76, f32[768]{0:T(1024)S(1)} %get-tuple-element.77, f32[768]{0:T(1024)S(1)} %get-tuple-element.78, ...), kind=kLoop, calls=%fused_computation.726 | loop fusion | flops 16257024 | bytes 11209728 | tf_op jit(solution)/shard_map/reshape | solution.py:115
  32.2 1.6 collective-permute-start.3
  33.8 3.0 %fusion.376 = bf16[144,768]{1,0:T(8,128)(2,1)S(1)} fusion(f32[768]{0:T(1024)S(1)} %copy-done.55, f32[768]{0:T(1024)S(1)} %copy-done.57, f32[768]{0:T(1024)S(1)} %get-tuple-element.74, f32[768]{0:T(1024)S(1)} %get-tuple-element.75, f32[768]{0:T(1024)S(1)} %get-tuple-element.76, f32[768]{0:T(1024)S(1)} %get-tuple-element.77, f32[768]{0:T(1024)S(1)} %get-tuple-element.78, ...), kind=kLoop, calls=%fused_computation.724 | loop fusion | flops 16257024 | bytes 11209728 | tf_op jit(solution)/shard_map/reshape | solution.py:115
  37.3 3.0 %fusion.377 = bf16[144,768]{1,0:T(8,128)(2,1)S(1)} fusion(f32[768]{0:T(1024)S(1)} %copy-done.55, bf16[9,150,768]{2,1,0:T(8,128)(2,1)S(1)} %fusion.26, f32[768]{0:T(1024)S(1)} %copy-done.57, f32[768]{0:T(1024)S(1)} %get-tuple-element.74, f32[768]{0:T(1024)S(1)} %get-tuple-element.75, bf16[3,144,768]{2,1,0:T(8,128)(2,1)S(1)} %copy-done.4, ...), kind=kLoop, calls=%fused_computation.725 | loop fusion | flops 16257024 | bytes 11209728 | tf_op jit(solution)/shard_map/reshape | solution.py:115
  40.3 1.6 collective-permute-start.5
  41.9 6.0 %fusion.386 = f32[864,1536]{1,0:T(8,128)S(1)} fusion(bf16[1536,1536]{1,0:T(8,128)(2,1)S(1)} %bitcast.104, bf16[432,1536]{1,0:T(8,128)(2,1)} %collective-permute-done.2, bf16[432,1536]{1,0:T(8,128)(2,1)} %fusion.17), kind=kOutput, calls=%fused_computation.809 | convolution fusion | flops 4082171904 | bytes 12681216 | tf_op jit(solution)/shard_map/dot_general | solution.py:104
  48.0 2.0 collective-permute-done.5
  52.0 2.9 %collective-permute-done.6 = bf16[432,1536]{1,0:T(8,128)(2,1)S(1)} collective-permute-done((bf16[432,1536]{1,0:T(8,128)(2,1)S(1)}, bf16[432,1536]{1,0:T(8,128)(2,1)S(1)}, u32[]{:S(2)}, u32[]{:S(2)}) %collective-permute-start.6) | collective-permute-done | bytes 1327136 | tf_op jit(solution)/shard_map/ppermute | solution.py:140
  55.0 9.2 %fusion.8 = (bf16[864,1536]{1,0:T(8,128)(2,1)}, f32[864,1536]{1,0:T(8,128)S(1)}) fusion(f32[864,1536]{1,0:T(8,128)S(1)} %fusion.386, bf16[1536,1536]{1,0:T(8,128)(2,1)S(1)} %get-tuple-element.135, bf16[432,1536]{1,0:T(8,128)(2,1)S(1)} %collective-permute-done.6, bf16[432,1536]{1,0:T(8,128)(2,1)S(1)} %fusion.14), kind=kOutput, calls=%fused_computation.63 | convolution fusion | flops 4108713984 | bytes 20643840 | tf_op jit(solution)/shard_map/dot_general | solution.py:141
  64.2 9.0 %fusion.1 = bf16[1536,1536]{1,0:T(8,128)(2,1)} fusion(f32[864,1536]{1,0:T(8,128)S(1)} %get-tuple-element.133, bf16[432,1536]{1,0:T(8,128)(2,1)} %collective-permute-done.2, bf16[432,1536]{1,0:T(8,128)(2,1)} %fusion.17), kind=kOutput, calls=%fused_computation.54 | convolution fusion | flops 4098834432 | bytes 12681216 | tf_op jit(solution)/shard_map/dot_general | solution.py:146
  73.3 6.2 %convolution_convert_fusion = bf16[432,1536]{1,0:T(8,128)(2,1)} fusion(bf16[1536,1536]{1,0:T(8,128)(2,1)} %copy-done.11, bf16[864,1536]{1,0:T(8,128)(2,1)} %get-tuple-element.132), kind=kOutput, calls=%fused_computation.72 | convolution fusion | flops 2039095296 | bytes 7372800 | tf_op jit(solution)/shard_map/dot_general | solution.py:152
  79.6 1.4 dynamic_slice.23
  81.1 1.3 copy-done.5
  82.5 1.0 copy-done.12
  83.6 5.9 %multiply_reduce_fusion = (f32[432]{0:T(512)S(1)}, f32[432]{0:T(512)S(1)}, f32[432,1536]{1,0:T(8,128)S(1)}) fusion(f32[1536]{0:T(1024)S(1)} %copy-done.63, f32[432]{0:T(512)S(1)} %copy-done.65, f32[432]{0:T(512)S(1)} %copy-done.61, bf16[432,768]{1,0:T(8,128)(2,1)S(1)} %copy-done.10, bf16[432,768]{1,0:T(8,128)(2,1)S(1)} %copy-done.8, ...), kind=kOutput, calls=%fused_computation.85 | convolution fusion | flops 2046393600 | bytes 11367168 | tf_op jit(solution)/shard_map/dot_general | solution.py:152
  90.2 1.1 collective-permute-start.9
  91.4 1.0 collective-permute-start.8
  92.4 7.0 %fusion = bf16[1536,1536]{1,0:T(8,128)(2,1)} fusion(bf16[864,1536]{1,0:T(8,128)(2,1)S(1)} %copy-done.70, bf16[432,1536]{1,0:T(8,128)(2,1)S(1)} %copy-done.69, bf16[432,1536]{1,0:T(8,128)(2,1)S(1)} %copy-done.22), kind=kOutput, calls=%fused_computation.53 | convolution fusion | flops 4086890496 | bytes 10027008 | tf_op jit(solution)/shard_map/dot_general | solution.py:146
  100.1 8.5 %collective-permute-done.8 = bf16[432,768]{1,0:T(8,128)(2,1)} collective-permute-done((bf16[432,768]{1,0:T(8,128)(2,1)S(1)}, bf16[432,768]{1,0:T(8,128)(2,1)}, u32[]{:S(2)}, u32[]{:S(2)}) %collective-permute-start.8) | collective-permute-done | bytes 663584 | tf_op jit(solution)/shard_map/ppermute | solution.py:168
  108.7 2.3 multiply_convert_fusion.2
  111.2 3.2 %fusion.74 = (f32[768]{0:T(1024)S(1)}, f32[768]{0:T(1024)S(1)}, f32[768]{0:T(1024)S(1)}, f32[768]{0:T(1024)S(1)}, f32[768]{0:T(1024)S(1)}, /*index=5*/f32[768]{0...) fusion(bf16[3,144,768]{2,1,0:T(8,128)(2,1)S(1)} %bitcast.97, ...), kind=kLoop, calls=%fused_computation.140 | loop fusion | flops 13261056 | bytes 9329664 | tf_op jit(solution)/shard_map/reduce_sum | solution.py:50
  114.5 3.2 %fusion.75 = (f32[768]{0:T(1024)S(1)}, f32[768]{0:T(1024)S(1)}, f32[768]{0:T(1024)S(1)}, f32[768]{0:T(1024)S(1)}, f32[768]{0:T(1024)S(1)}, /*index=5*/f32[768]{0...) fusion(bf16[3,144,768]{2,1,0:T(8,128)(2,1)S(1)} %bitcast.98, ...), kind=kLoop, calls=%fused_computation.141 | loop fusion | flops 18233856 | bytes 12662784 | tf_op jit(solution)/shard_map/reduce_sum | solution.py:50
  117.8 3.3 %fusion.76 = (f32[768]{0:T(1024)S(1)}, f32[768]{0:T(1024)S(1)}, f32[768]{0:T(1024)S(1)}, f32[768]{0:T(1024)S(1)}, f32[768]{0:T(1024)S(1)}, /*index=5*/f32[768]{0...) fusion(bf16[3,144,768]{2,1,0:T(8,128)(2,1)S(1)} %bitcast.99, ...), kind=kLoop, calls=%fused_computation.142 | loop fusion | flops 18233856 | bytes 12662784 | tf_op jit(solution)/shard_map/reduce_sum | solution.py:50
  122.1 1.3 collective-permute-done.14
  123.4 1.6 collective-permute-start.15
  125.0 3.7 %collective-permute-done.15 = bf16[7,7,768]{2,1,0:T(8,128)(2,1)S(1)} collective-permute-done((bf16[7,7,768]{2,1,0:T(8,128)(2,1)S(1)}, bf16[7,7,768]{2,1,0:T(8,128)(2,1)S(1)}, u32[]{:S(2)}, u32[]{:S(2)}) %collective-permute-start.15) | collective-permute-done | bytes 75296 | tf_op jit(solution)/shard_map/ppermute | solution.py:201
  128.7 1.6 collective-permute-start.16
  130.3 1.3 collective-permute-start.10
  131.6 1.3 collective-permute-start.11
  133.3 6.2 %collective-permute-start.17 = (bf16[7,7,768]{2,1,0:T(8,128)(2,1)S(1)}, bf16[7,7,768]{2,1,0:T(8,128)(2,1)S(1)}, u32[]{:S(2)}, u32[]{:S(2)}) collective-permute-start(bf16[7,7,768]{2,1,0:T(8,128)(2,1)S(1)} %add_convert_fusion), channel_id=1, source_target_pairs={{0,16},{2,18},{4,20},{6,22},{8,24},{10,26},{12,28},{14,30},{16,0},... | collective-permute-start | bytes 225800 | tf_op jit(solution)/shard_map/ppermute | solution.py:201
  139.5 1.2 dynamic-slice_convert_fusion.1
  140.7 9.2 %collective-permute-done.17 = bf16[7,7,768]{2,1,0:T(8,128)(2,1)S(1)} collective-permute-done((bf16[7,7,768]{2,1,0:T(8,128)(2,1)S(1)}, bf16[7,7,768]{2,1,0:T(8,128)(2,1)S(1)}, u32[]{:S(2)}, u32[]{:S(2)}) %collective-permute-start.17) | collective-permute-done | bytes 75296 | tf_op jit(solution)/shard_map/ppermute | solution.py:201
  150.8 1.0 select_maximum_fusion
  152.0 3.2 %fusion.375 = bf16[1,144,768]{2,1,0:T(8,128)(2,1)S(1)} fusion(f32[3,144,768]{2,1,0:T(8,128)S(1)} %dynamic-slice_convert_fusion.1, bf16[9,150,768]{2,1,0:T(8,128)(2,1)S(1)} %select_maximum_fusion, bf16[3,144,768]{2,1,0:T(8,128)(2,1)S(1)} %collective-permute-done.10, f32[768]{0:T(1024)S(1)} %get-tuple-element.97, f32[768]{0:T(1024)S(1)} %get-tuple-element.104, ...), kind=kLoop, calls=%fused_computation.715 | loop fusion | flops 16367616 | bytes 11652096 | tf_op jit(solution)/shard_map/convert_element_type | solution.py:194
  155.2 3.2 %fusion.177 = bf16[1,144,768]{2,1,0:T(8,128)(2,1)S(1)} fusion(f32[3,144,768]{2,1,0:T(8,128)S(1)} %dynamic-slice_convert_fusion.1, f32[768]{0:T(1024)S(1)} %copy-done.32, f32[768]{0:T(1024)S(1)} %get-tuple-element.97, f32[768]{0:T(1024)S(1)} %get-tuple-element.104, f32[768]{0:T(1024)S(1)} %copy-done.56, f32[768]{0:T(1024)S(1)} %copy-done.58, ...), kind=kLoop, calls=%fused_computation.517 | loop fusion | flops 16367616 | bytes 11652096 | tf_op jit(solution)/shard_map/convert_element_type | solution.py:194
  158.4 3.2 %fusion.374 = bf16[1,144,768]{2,1,0:T(8,128)(2,1)S(1)} fusion(f32[3,144,768]{2,1,0:T(8,128)S(1)} %dynamic-slice_convert_fusion.1, bf16[9,150,768]{2,1,0:T(8,128)(2,1)S(1)} %select_maximum_fusion, bf16[3,144,768]{2,1,0:T(8,128)(2,1)S(1)} %collective-permute-done.11, f32[768]{0:T(1024)S(1)} %get-tuple-element.82, f32[768]{0:T(1024)S(1)} %copy-done.32, ...), kind=kLoop, calls=%fused_computation.714 | loop fusion | flops 16367616 | bytes 11652096 | tf_op jit(solution)/shard_map/convert_element_type | solution.py:194
  162.5 15.6 %reduce-scatter.5.cloned.1.call-done = bf16[192,1536]{1,0:T(8,128)(2,1)} async-done(((bf16[1536,1536]{1,0:T(8,128)(2,1)}), bf16[192,1536]{1,0:T(8,128)(2,1)}) %reduce-scatter.5.cloned.1.call-update) | async-done | bytes 589840 | tf_op jit(solution)/shard_map/reduce_scatter | solution.py:65
  178.0 1.1 broadcast_select_fusion.4
  179.3 97.5 %reduce-scatter.3.cloned.1.call-done = bf16[192,1536]{1,0:T(8,128)(2,1)} async-done(((bf16[1536,1536]{1,0:T(8,128)(2,1)}), bf16[192,1536]{1,0:T(8,128)(2,1)}) %reduce-scatter.3.cloned.1.call-update) | async-done | bytes 589840 | tf_op jit(solution)/shard_map/reduce_scatter | solution.py:65
  276.8 1.1 broadcast_select_fusion.8
  278.0 1.1 convert_bitcast_fusion
  279.6 1.1 maximum_convert_fusion
  (257 shorter events, 10.7 us)
Async XLA Ops:
  7.2 9.7 %copy-start.59 = (f32[7,7,768]{2,1,0:T(8,128)S(1)}, f32[7,7,768]{2,1,0:T(8,128)}, u32[]{:S(2)}) copy-start(f32[7,7,768]{2,1,0:T(8,128)} %param.8) | copy-start | bytes 451588
  7.2 170.9 %reduce-scatter.5.cloned.1.call-start = ((), (), s32[]{:S(2)}) async-start(), calls=%async_computation.3 | async-start | bytes 5308416 | tf_op jit(solution)/shard_map/reduce_scatter | solution.py:65
  7.2 17.8 %collective-permute-start = (bf16[3,144,768]{2,1,0:T(8,128)(2,1)}, bf16[3,144,768]{2,1,0:T(8,128)(2,1)S(1)}, u32[]{:S(2)}, u32[]{:S(2)}) collective-permute-start(bf16[3,144,768]{2,1,0:T(8,128)(2,1)} %param.7), channel_id=1, source_target_pairs={{0,2},{2,4},{4,6},{6,8},{8,10},{10,12},{12,14},{14,16},{16,18},{18... | collective-permute-start | bytes 1990664 | tf_op jit(solution)/shard_map/ppermute | solution.py:14
  9.8 15.3 %collective-permute-start.1 = (bf16[3,144,768]{2,1,0:T(8,128)(2,1)}, bf16[3,144,768]{2,1,0:T(8,128)(2,1)S(1)}, u32[]{:S(2)}, u32[]{:S(2)}) collective-permute-start(bf16[3,144,768]{2,1,0:T(8,128)(2,1)} %param.7), channel_id=1, source_target_pairs={{2,0},{4,2},{6,4},{8,6},{10,8},{12,10},{14,12},{16,14},{18,16},{20... | collective-permute-start | bytes 1990664 | tf_op jit(solution)/shard_map/ppermute | solution.py:15
  13.7 28.2 %collective-permute-start.2 = (bf16[432,1536]{1,0:T(8,128)(2,1)}, bf16[432,1536]{1,0:T(8,128)(2,1)}, u32[]{:S(2)}, u32[]{:S(2)}) collective-permute-start(bf16[432,1536]{1,0:T(8,128)(2,1)} %fusion.17), channel_id=1, source_target_pairs={{0,2},{2,0},{4,6},{6,4},{8,10},{10,8},{12,14},{14,12},{16,18},{18,... | collective-permute-start | bytes 3981320 | tf_op jit(solution)/shard_map/ppermute | solution.py:101
  18.5 7.5 %copy-start = (bf16[3,144,768]{2,1,0:T(8,128)(2,1)S(1)}, bf16[3,144,768]{2,1,0:T(8,128)(2,1)}, u32[]{:S(2)}) copy-start(bf16[3,144,768]{2,1,0:T(8,128)(2,1)} %param.7) | copy-start | bytes 1990660
  25.1 29.9 %copy-start.11 = (bf16[1536,1536]{1,0:T(8,128)(2,1)}, bf16[1536,1536]{1,0:T(8,128)(2,1)S(1)}, u32[]{:S(2)}) copy-start(bf16[1536,1536]{1,0:T(8,128)(2,1)S(1)} %get-tuple-element.135) | copy-start | bytes 14155780
  25.1 55.8 %copy-start.1 = (bf16[3,144,768]{2,1,0:T(8,128)(2,1)}, bf16[3,144,768]{2,1,0:T(8,128)(2,1)S(1)}, u32[]{:S(2)}) copy-start(bf16[3,144,768]{2,1,0:T(8,128)(2,1)S(1)} %collective-permute-done) | copy-start | bytes 1990660
  26.0 2.9 %copy-start.27 = (f32[768]{0:T(1024)S(1)}, f32[768]{0:T(1024)}, u32[]{:S(2)}) copy-start(f32[768]{0:T(1024)} %get-tuple-element.87) | copy-start | bytes 9220
  26.0 2.9 %copy-start.29 = (f32[768]{0:T(1024)S(1)}, f32[768]{0:T(1024)}, u32[]{:S(2)}) copy-start(f32[768]{0:T(1024)} %get-tuple-element.88) | copy-start | bytes 9220
  26.0 2.9 %copy-start.31 = (f32[768]{0:T(1024)S(1)}, f32[768]{0:T(1024)}, u32[]{:S(2)}) copy-start(f32[768]{0:T(1024)} %get-tuple-element.89) | copy-start | bytes 9220
  26.0 2.9 %copy-start.33 = (f32[768]{0:T(1024)S(1)}, f32[768]{0:T(1024)}, u32[]{:S(2)}) copy-start(f32[768]{0:T(1024)} %get-tuple-element.90) | copy-start | bytes 9220
  26.0 2.9 %copy-start.35 = (f32[768]{0:T(1024)S(1)}, f32[768]{0:T(1024)}, u32[]{:S(2)}) copy-start(f32[768]{0:T(1024)} %get-tuple-element.91) | copy-start | bytes 9220
  26.0 2.9 %copy-start.37 = (f32[768]{0:T(1024)S(1)}, f32[768]{0:T(1024)}, u32[]{:S(2)}) copy-start(f32[768]{0:T(1024)} %get-tuple-element.111) | copy-start | bytes 9220
  26.0 2.9 %copy-start.39 = (f32[768]{0:T(1024)S(1)}, f32[768]{0:T(1024)}, u32[]{:S(2)}) copy-start(f32[768]{0:T(1024)} %get-tuple-element.112) | copy-start | bytes 9220
  26.0 2.9 %copy-start.41 = (f32[768]{0:T(1024)S(1)}, f32[768]{0:T(1024)}, u32[]{:S(2)}) copy-start(f32[768]{0:T(1024)} %get-tuple-element.113) | copy-start | bytes 9220
  26.0 2.9 %copy-start.43 = (f32[768]{0:T(1024)S(1)}, f32[768]{0:T(1024)}, u32[]{:S(2)}) copy-start(f32[768]{0:T(1024)} %get-tuple-element.114) | copy-start | bytes 9220
  26.1 2.9 %copy-start.45 = (f32[768]{0:T(1024)S(1)}, f32[768]{0:T(1024)}, u32[]{:S(2)}) copy-start(f32[768]{0:T(1024)} %get-tuple-element.115) | copy-start | bytes 9220
  26.1 2.9 %copy-start.47 = (f32[768]{0:T(1024)S(1)}, f32[768]{0:T(1024)}, u32[]{:S(2)}) copy-start(f32[768]{0:T(1024)} %get-tuple-element.116) | copy-start | bytes 9220
  26.1 2.9 %copy-start.49 = (f32[768]{0:T(1024)S(1)}, f32[768]{0:T(1024)}, u32[]{:S(2)}) copy-start(f32[768]{0:T(1024)} %get-tuple-element.117) | copy-start | bytes 9220
  26.1 2.9 %copy-start.51 = (f32[768]{0:T(1024)S(1)}, f32[768]{0:T(1024)}, u32[]{:S(2)}) copy-start(f32[768]{0:T(1024)} %get-tuple-element.118) | copy-start | bytes 9220
  26.1 2.9 %copy-start.53 = (f32[768]{0:T(1024)S(1)}, f32[768]{0:T(1024)}, u32[]{:S(2)}) copy-start(f32[768]{0:T(1024)} %get-tuple-element.119) | copy-start | bytes 9220
  29.1 12.9 %slice-start = ((s8[4718592]{0:T(1024)(128)(4,1)}), s8[4194304]{0:T(1024)(128)(4,1)S(1)}, s32[]{:S(2)}) async-start(s8[4718592]{0:T(1024)(128)(4,1)} %bitcast.103), calls=%async_computation.4 | async-start | bytes 8388608
  32.2 17.8 %copy-start.17 = (bf16[144,768]{1,0:T(8,128)(2,1)}, bf16[144,768]{1,0:T(8,128)(2,1)S(1)}, u32[]{:S(2)}) copy-start(bf16[144,768]{1,0:T(8,128)(2,1)S(1)} %fusion.378) | copy-start | bytes 663556
  32.2 9.7 %slice-start.1 = ((s8[4718592]{0:T(1024)(128)(4,1)}), s8[524288]{0:T(1024)(128)(4,1)S(1)}, s32[]{:S(2)}) async-start(s8[4718592]{0:T(1024)(128)(4,1)} %bitcast.103), calls=%async_computation.5 | async-start | bytes 1048576
  32.2 17.7 %collective-permute-start.3 = (bf16[144,768]{1,0:T(8,128)(2,1)S(1)}, bf16[144,768]{1,0:T(8,128)(2,1)S(1)}, u32[]{:S(2)}, u32[]{:S(2)}) collective-permute-start(bf16[144,768]{1,0:T(8,128)(2,1)S(1)} %fusion.378), channel_id=1, source_target_pairs={{0,1},{1,0},{2,3},{3,2},{4,5},{5,4},{6,7},{7,6},{8,9},{9,8},{10,11... | collective-permute-start | bytes 663560 | tf_op jit(solution)/shard_map/ppermute | solution.py:120
  36.7 13.3 %copy-start.18 = (bf16[144,768]{1,0:T(8,128)(2,1)}, bf16[144,768]{1,0:T(8,128)(2,1)S(1)}, u32[]{:S(2)}) copy-start(bf16[144,768]{1,0:T(8,128)(2,1)S(1)} %fusion.376) | copy-start | bytes 663556
  36.7 13.2 %collective-permute-start.4 = (bf16[144,768]{1,0:T(8,128)(2,1)S(1)}, bf16[144,768]{1,0:T(8,128)(2,1)S(1)}, u32[]{:S(2)}, u32[]{:S(2)}) collective-permute-start(bf16[144,768]{1,0:T(8,128)(2,1)S(1)} %fusion.376), channel_id=1, source_target_pairs={{0,1},{1,0},{2,3},{3,2},{4,5},{5,4},{6,7},{7,6},{8,9},{9,8},{10,11... | collective-permute-start | bytes 663560 | tf_op jit(solution)/shard_map/ppermute | solution.py:120
  40.3 9.7 %copy-start.19 = (bf16[144,768]{1,0:T(8,128)(2,1)}, bf16[144,768]{1,0:T(8,128)(2,1)S(1)}, u32[]{:S(2)}) copy-start(bf16[144,768]{1,0:T(8,128)(2,1)S(1)} %fusion.377) | copy-start | bytes 663556
  40.3 9.6 %collective-permute-start.5 = (bf16[144,768]{1,0:T(8,128)(2,1)S(1)}, bf16[144,768]{1,0:T(8,128)(2,1)S(1)}, u32[]{:S(2)}, u32[]{:S(2)}) collective-permute-start(bf16[144,768]{1,0:T(8,128)(2,1)S(1)} %fusion.377), channel_id=1, source_target_pairs={{0,1},{1,0},{2,3},{3,2},{4,5},{5,4},{6,7},{7,6},{8,9},{9,8},{10,11... | collective-permute-start | bytes 663560 | tf_op jit(solution)/shard_map/ppermute | solution.py:120
  51.9 12.2 %copy-start.21 = (bf16[432,1536]{1,0:T(8,128)(2,1)}, bf16[432,1536]{1,0:T(8,128)(2,1)S(1)}, u32[]{:S(2)}) copy-start(bf16[432,1536]{1,0:T(8,128)(2,1)S(1)} %fusion.14) | copy-start | bytes 3981316
  51.9 3.1 %collective-permute-start.6 = (bf16[432,1536]{1,0:T(8,128)(2,1)S(1)}, bf16[432,1536]{1,0:T(8,128)(2,1)S(1)}, u32[]{:S(2)}, u32[]{:S(2)}) collective-permute-start(bf16[432,1536]{1,0:T(8,128)(2,1)S(1)} %fusion.14), channel_id=1, source_target_pairs={{0,2},{2,0},{4,6},{6,4},{8,10},{10,8},{12,14},{14,12},{16,18},{18,... | collective-permute-start | bytes 3981320 | tf_op jit(solution)/shard_map/ppermute | solution.py:140
  55.0 9.2 %copy-start.68 = (bf16[432,1536]{1,0:T(8,128)(2,1)}, bf16[432,1536]{1,0:T(8,128)(2,1)S(1)}, u32[]{:S(2)}) copy-start(bf16[432,1536]{1,0:T(8,128)(2,1)S(1)} %collective-permute-done.6) | copy-start | bytes 3981316
  73.2 203.5 %reduce-scatter.3.cloned.1.call-start = ((), (), s32[]{:S(2)}) async-start(), calls=%async_computation.2 | async-start | bytes 5308416 | tf_op jit(solution)/shard_map/reduce_scatter | solution.py:65
  79.4 4.1 %collective-permute-start.7 = (bf16[432,1536]{1,0:T(8,128)(2,1)}, bf16[432,1536]{1,0:T(8,128)(2,1)}, u32[]{:S(2)}, u32[]{:S(2)}) collective-permute-start(bf16[432,1536]{1,0:T(8,128)(2,1)} %convolution_convert_fusion), channel_id=1, source_target_pairs={{0,2},{2,0},{4,6},{6,4},{8,10},{10,8},{12,14},{14,12},{16,18},{18,... | collective-permute-start | bytes 3981320 | tf_op jit(solution)/shard_map/ppermute | solution.py:157
  83.6 8.8 %copy-start.69 = (bf16[432,1536]{1,0:T(8,128)(2,1)S(1)}, bf16[432,1536]{1,0:T(8,128)(2,1)}, u32[]{:S(2)}) copy-start(bf16[432,1536]{1,0:T(8,128)(2,1)} %copy-done.68) | copy-start | bytes 3981316
  83.6 8.8 %copy-start.70 = (bf16[864,1536]{1,0:T(8,128)(2,1)S(1)}, bf16[864,1536]{1,0:T(8,128)(2,1)}, u32[]{:S(2)}) copy-start(bf16[864,1536]{1,0:T(8,128)(2,1)} %get-tuple-element.132) | copy-start | bytes 7962628
  90.2 9.2 %collective-permute-start.9 = (f32[2,432]{1,0:T(2,128)}, f32[2,432]{1,0:T(2,128)}, u32[]{:S(2)}, u32[]{:S(2)}) collective-permute-start(f32[2,432]{1,0:T(2,128)} %pad_maximum_fusion.7), channel_id=1, source_target_pairs={{0,1},{1,0},{2,3},{3,2},{4,5},{5,4},{6,7},{7,6},{8,9},{9,8},{10,11... | collective-permute-start | bytes 10376 | tf_op jit(solution)/shard_map/ppermute | solution.py:170
  91.4 17.3 %collective-permute-start.8 = (bf16[432,768]{1,0:T(8,128)(2,1)S(1)}, bf16[432,768]{1,0:T(8,128)(2,1)}, u32[]{:S(2)}, u32[]{:S(2)}) collective-permute-start(bf16[432,768]{1,0:T(8,128)(2,1)S(1)} %dynamic-slice_convert_fusion), channel_id=1, source_target_pairs={{0,1},{1,0},{2,3},{3,2},{4,5},{5,4},{6,7},{7,6},{8,9},{9,8},{10,11... | collective-permute-start | bytes 1990664 | tf_op jit(solution)/shard_map/ppermute | solution.py:168
  122.0 1.3 collective-permute-start.14
  123.4 5.3 %collective-permute-start.15 = (bf16[7,7,768]{2,1,0:T(8,128)(2,1)S(1)}, bf16[7,7,768]{2,1,0:T(8,128)(2,1)S(1)}, u32[]{:S(2)}, u32[]{:S(2)}) collective-permute-start(bf16[7,7,768]{2,1,0:T(8,128)(2,1)S(1)} %add_convert_fusion.2), channel_id=1, source_target_pairs={{0,4},{2,6},{4,0},{6,2},{8,12},{10,14},{12,8},{14,10},{16,20},{18,... | collective-permute-start | bytes 225800 | tf_op jit(solution)/shard_map/ppermute | solution.py:201
  128.7 4.6 %collective-permute-start.16 = (bf16[7,7,768]{2,1,0:T(8,128)(2,1)S(1)}, bf16[7,7,768]{2,1,0:T(8,128)(2,1)S(1)}, u32[]{:S(2)}, u32[]{:S(2)}) collective-permute-start(bf16[7,7,768]{2,1,0:T(8,128)(2,1)S(1)} %add_convert_fusion.1), channel_id=1, source_target_pairs={{0,8},{2,10},{4,12},{6,14},{8,0},{10,2},{12,4},{14,6},{16,24},{18,... | collective-permute-start | bytes 225800 | tf_op jit(solution)/shard_map/ppermute | solution.py:201
  130.3 20.5 %collective-permute-start.10 = (bf16[3,144,768]{2,1,0:T(8,128)(2,1)S(1)}, bf16[3,144,768]{2,1,0:T(8,128)(2,1)S(1)}, u32[]{:S(2)}, u32[]{:S(2)}) collective-permute-start(bf16[3,144,768]{2,1,0:T(8,128)(2,1)S(1)} %bitcast.100), channel_id=1, source_target_pairs={{0,2},{2,4},{4,6},{6,8},{8,10},{10,12},{12,14},{14,16},{16,18},{18... | collective-permute-start | bytes 1990664 | tf_op jit(solution)/shard_map/ppermute | solution.py:14
  131.6 19.2 %collective-permute-start.11 = (bf16[3,144,768]{2,1,0:T(8,128)(2,1)S(1)}, bf16[3,144,768]{2,1,0:T(8,128)(2,1)S(1)}, u32[]{:S(2)}, u32[]{:S(2)}) collective-permute-start(bf16[3,144,768]{2,1,0:T(8,128)(2,1)S(1)} %bitcast.101), channel_id=1, source_target_pairs={{2,0},{4,2},{6,4},{8,6},{10,8},{12,10},{14,12},{16,14},{18,16},{20... | collective-permute-start | bytes 1990664 | tf_op jit(solution)/shard_map/ppermute | solution.py:15
  133.3 16.6 %collective-permute-start.17 = (bf16[7,7,768]{2,1,0:T(8,128)(2,1)S(1)}, bf16[7,7,768]{2,1,0:T(8,128)(2,1)S(1)}, u32[]{:S(2)}, u32[]{:S(2)}) collective-permute-start(bf16[7,7,768]{2,1,0:T(8,128)(2,1)S(1)} %add_convert_fusion), channel_id=1, source_target_pairs={{0,16},{2,18},{4,20},{6,22},{8,24},{10,26},{12,28},{14,30},{16,0},... | collective-permute-start | bytes 225800 | tf_op jit(solution)/shard_map/ppermute | solution.py:201
  178.0 99.9 %copy-start.15 = (bf16[192,1536]{1,0:T(8,128)(2,1)S(1)}, bf16[192,1536]{1,0:T(8,128)(2,1)}, u32[]{:S(2)}) copy-start(bf16[192,1536]{1,0:T(8,128)(2,1)} %reduce-scatter.5.cloned.1.call-done) | copy-start | bytes 1769476
  179.2 98.7 %collective-permute-start.13 = (bf16[96,1536]{1,0:T(8,128)(2,1)S(1)}, bf16[96,1536]{1,0:T(8,128)(2,1)S(1)}, u32[]{:S(2)}, u32[]{:S(2)}) collective-permute-start(bf16[96,1536]{1,0:T(8,128)(2,1)S(1)} %broadcast_select_fusion.4), channel_id=1, source_target_pairs={{0,2},{2,0},{4,6},{6,4},{8,10},{10,8},{12,14},{14,12},{16,18},{18,... | collective-permute-start | bytes 884744 | tf_op jit(solution)/shard_map/ppermute | solution.py:75
  277.9 1.6 collective-permute-start.12
  (45 other events, 77.9 us)
Sparse Core Ops, SparseCore 0:
  73.3 104.6 reduce-scatter.4
  181.7 95.0 reduce-scatter.2
